TPU v7x, 256 devices: a whole 4x4x8 slice. The times are simulated.
256 devices in a mesh: tm: 4 (over z_lo, core), space: 64 (over x, y, z_hi).
Axes of the slice: x: 4, y: 4, z: 8 (z_hi: 4, z_lo: 2; z = z_hi * 2 + z_lo), core: 2. Of those that a mesh axis runs over, the one named last changes fastest.
Arguments:
- trajectory: float32 [8, 4, 512, 512], P('tm', None, 'space'), may hold values from -6 to 6
- noise: float32 [8, 4, 512, 512], P('tm', None, 'space'), may hold values from -6 to 6
- step_size: float32 [8], P('tm'), may hold values from 0.2 to 0.6
- noise_scale: float32 [8], P('tm'), may hold values from 0.2 to 0.5
- time_bias: float32 [8, 128], P('tm'), may hold values from -5 to 5
- start_state: float32 [4, 512, 512], P(None, 'space'), may hold values from -6 to 6
- observed: float32 [4, 512, 512], P(None, 'space'), may hold values from -6 to 6
- conv_in: bfloat16 [9, 128, 4], replicated, may hold values from -1 to 1
- conv_mid: bfloat16 [9, 128, 128], replicated, may hold values from -0.1875 to 0.1875
- conv_out: bfloat16 [9, 4, 128], replicated, may hold values from -0.1875 to 0.1875
- psf_bank: float32 [16, 4, 25], replicated, may hold values from 0.02 to 0.12
- index_map: int32 [64, 64], replicated, may hold values from 0 to 15
Outputs:
- new_trajectory: float32 [8, 4, 512, 512], P('tm', None, 'space')
All inputs are finite; a program needn't handle non-finite values.
Results may differ from a plain program's by a relative error of at most 0.0024.
Values may be sent and summed in bfloat16 or wider, within the bound.
No kernel may reach another device: no remote copies, remote signals or barrier semaphores. Data moves between devices by JAX's collectives and lax.ppermute only.
A program may use at most 128 MiB of HBM per device.

v0:
```python
import jax
import jax.numpy as jnp
from jax import lax
from jax.sharding import PartitionSpec as P

NPSF = 16
BLOCK = 8


def with_halo(cells, sides, width):
    for axis, dim in sides:
        count = lax.axis_size(axis)
        ends = count - 1
        head = lax.slice_in_dim(cells, 0, width, axis=dim)
        tail = lax.slice_in_dim(cells, cells.shape[dim] - width, cells.shape[dim], axis=dim)
        cells = jnp.concatenate(
            [
                lax.ppermute(tail, axis, [(i, (i + 1) % count) for i in range(ends)]),
                cells,
                lax.ppermute(head, axis, [((i + 1) % count, i) for i in range(ends)]),
            ],
            axis=dim,
        )
    return cells


def entering(part, axis, combine, identity):
    place = lax.axis_index(axis)
    gathered = lax.all_gather(part, axis)
    state = jnp.zeros_like(part) + jnp.asarray(identity, part.dtype)

    def one(hop, state):
        return combine(state, lax.dynamic_index_in_dim(gathered, hop, 0, False))

    return lax.fori_loop(0, place, one, state)


def conv_stacked_in(source, kernel):
    chans = source.shape[0]
    out_rows = source.shape[1] - 2
    width = source.shape[2]
    padded = jnp.pad(source, ((0, 0), (0, 0), (1, 1)))
    windows = jnp.concatenate(
        [
            padded[:, tap // 3 : tap // 3 + out_rows, tap % 3 : tap % 3 + width].reshape(
                chans, out_rows * width
            )
            for tap in range(9)
        ],
        axis=0,
    )
    flat_kernel = jnp.transpose(kernel, (1, 0, 2)).reshape(kernel.shape[1], 9 * chans)
    total = jnp.dot(flat_kernel, windows, preferred_element_type=jnp.float32)
    return total.reshape(kernel.shape[1], out_rows, width)


def conv_stacked_out(source, kernel):
    chans = source.shape[0]
    out_rows = source.shape[1] - 2
    width = source.shape[2]
    outs = kernel.shape[1]
    padded = jnp.pad(source, ((0, 0), (0, 0), (1, 1)))
    flat_kernel = kernel.reshape(9 * outs, chans)
    product = jnp.dot(
        flat_kernel,
        padded.reshape(chans, (out_rows + 2) * (width + 2)),
        preferred_element_type=jnp.float32,
    )
    product = product.reshape(9, outs, out_rows + 2, width + 2)
    total = jnp.zeros((outs, out_rows, width), jnp.float32)
    for tap in range(9):
        row_off = tap // 3
        col_off = tap % 3
        total = total + product[tap, :, row_off : row_off + out_rows, col_off : col_off + width]
    return total


def blur_forward(field_ext, weights, out_rows):
    width = field_ext.shape[2]
    padded = jnp.pad(field_ext, ((0, 0), (0, 0), (2, 2)))
    total = jnp.zeros((field_ext.shape[0], out_rows, width), jnp.float32)
    for tap in range(25):
        row_off = tap // 5
        col_off = tap % 5
        total = (
            total
            + weights[:, tap] * padded[:, row_off : row_off + out_rows, col_off : col_off + width]
        )
    return total


def blur_adjoint(misfit_ext, weights, out_rows):
    width = misfit_ext.shape[2]
    total = jnp.zeros((misfit_ext.shape[0], out_rows, width), jnp.float32)
    for tap in range(25):
        row_off = tap // 5
        col_off = tap % 5
        padded = jnp.pad(weights[:, tap] * misfit_ext, ((0, 0), (0, 0), (2, 2)))
        total = (
            total
            + padded[:, 4 - row_off : 4 - row_off + out_rows, 4 - col_off : 4 - col_off + width]
        )
    return total


def per_device(
    trajectory,
    noise,
    step_size,
    noise_scale,
    time_bias,
    start_state,
    observed,
    conv_in,
    conv_mid,
    conv_out,
    psf_bank,
    index_map,
):
    rows = observed.shape[1]
    steps_here = trajectory.shape[0]
    position = lax.axis_index("space")
    padded_map = jnp.pad(index_map, ((1, 1), (0, 0)))
    block_rows = lax.dynamic_slice_in_dim(
        padded_map, position * (rows // BLOCK), rows // BLOCK + 2, 0
    )
    pixel_map = jnp.repeat(jnp.repeat(block_rows, BLOCK, axis=0), BLOCK, axis=1)[
        BLOCK - 2 : BLOCK + rows + 2
    ]
    one_hot = (pixel_map[None] == jnp.arange(NPSF, dtype=jnp.int32)[:, None, None]).astype(
        jnp.float32
    )
    weights = jnp.einsum("kbt,krw->btrw", psf_bank, one_hot, precision=lax.Precision.HIGHEST)
    running = jnp.zeros(start_state.shape, jnp.float32)
    partials = []
    for moment in range(steps_here):
        state = trajectory[moment]
        bias = time_bias[moment][:, None, None]
        state_ext = with_halo(state.astype(jnp.bfloat16), (("space", 1),), 2).astype(state.dtype)
        first_pre = conv_stacked_in(state_ext[:, 1 : rows + 3].astype(jnp.bfloat16), conv_in)
        hidden_one = jax.nn.silu(first_pre + bias).astype(jnp.bfloat16)
        one_ext = with_halo(hidden_one, (("space", 1),), 1)
        second_pre = conv_stacked_in(one_ext, conv_mid)
        hidden_two = (hidden_one.astype(jnp.float32) + jax.nn.silu(second_pre)).astype(jnp.bfloat16)
        two_ext = with_halo(hidden_two, (("space", 1),), 1)
        score = conv_stacked_out(two_ext, conv_out)
        blurred = blur_forward(state_ext, weights[:, :, 2 : rows + 2], rows)
        misfit_ext = with_halo(
            (observed - blurred).astype(jnp.bfloat16), (("space", 1),), 2
        ).astype(jnp.float32)
        guidance = blur_adjoint(misfit_ext, weights, rows)
        drift = step_size[moment] * (score + guidance) + noise_scale[moment] * noise[moment]
        running = running + drift
        partials.append(running)

    def add_terms(earlier_sum, later_sum):
        return earlier_sum + later_sum

    before = entering(running, "tm", add_terms, jnp.zeros(running.shape, jnp.float32))
    return jnp.stack([start_state + before + partial_sum for partial_sum in partials], axis=0)


def solution(mesh):
    return jax.shard_map(
        per_device,
        mesh=mesh,
        in_specs=(
            P("tm", None, "space", None),
            P("tm", None, "space", None),
            P("tm"),
            P("tm"),
            P("tm", None),
            P(None, "space", None),
            P(None, "space", None),
            P(),
            P(),
            P(),
            P(),
            P(),
        ),
        out_specs=P("tm", None, "space", None),
        check_vma=False,
    )
```

profile of v0, /device:TPU:7, one launch (start us, length us, event | category | flops | bytes accessed | tf_op | source)
XLA Modules:
  0.0 160.5 jit_solution(4404970218161342900)
XLA Ops:
  1.7 4.9 %collective-permute-start = (bf16[4,2,512]{2,0,1:T(4,128)(2,1)S(1)}, bf16[4,2,512]{2,0,1:T(4,128)(2,1)S(1)}, u32[]{:S(2)}, u32[]{:S(2)}) collective-permute-start(bf16[4,2,512]{2,0,1:T(4,128)(2,1)S(1)} %get-tuple-element.227), channel_id=1, source_target_pairs={{0,1},{1,2},{2,3},{3,4},{4,5},{5,6},{6,7},{7,8},{8,9},{9,10},{10,1... | collective-permute-start | bytes 24584 | tf_op jit(solution)/shard_map/ppermute | solution.py:18
  6.6 7.7 %collective-permute-start.1 = (bf16[4,2,512]{2,0,1:T(4,128)(2,1)S(1)}, bf16[4,2,512]{2,0,1:T(4,128)(2,1)S(1)}, u32[]{:S(2)}, u32[]{:S(2)}) collective-permute-start(bf16[4,2,512]{2,0,1:T(4,128)(2,1)S(1)} %get-tuple-element.228), channel_id=1, source_target_pairs={{1,0},{2,1},{3,2},{4,3},{5,4},{6,5},{7,6},{8,7},{9,8},{10,9},{11,1... | collective-permute-start | bytes 24584 | tf_op jit(solution)/shard_map/ppermute | solution.py:20
  14.3 1.9 %collective-permute-start.8 = (bf16[4,2,512]{2,0,1:T(4,128)(2,1)S(1)}, bf16[4,2,512]{2,0,1:T(4,128)(2,1)S(1)}, u32[]{:S(2)}, u32[]{:S(2)}) collective-permute-start(bf16[4,2,512]{2,0,1:T(4,128)(2,1)S(1)} %get-tuple-element.233), channel_id=1, source_target_pairs={{0,1},{1,2},{2,3},{3,4},{4,5},{5,6},{6,7},{7,8},{8,9},{9,10},{10,1... | collective-permute-start | bytes 24584 | tf_op jit(solution)/shard_map/ppermute | solution.py:18
  16.2 8.5 %collective-permute-start.9 = (bf16[4,2,512]{2,0,1:T(4,128)(2,1)S(1)}, bf16[4,2,512]{2,0,1:T(4,128)(2,1)S(1)}, u32[]{:S(2)}, u32[]{:S(2)}) collective-permute-start(bf16[4,2,512]{2,0,1:T(4,128)(2,1)S(1)} %get-tuple-element.234), channel_id=1, source_target_pairs={{1,0},{2,1},{3,2},{4,3},{5,4},{6,5},{7,6},{8,7},{9,8},{10,9},{11,1... | collective-permute-start | bytes 24584 | tf_op jit(solution)/shard_map/ppermute | solution.py:20
  25.8 2.4 %convolution_bitcast_fusion.2 = f32[4,25,12,512]{3,1,0,2:T(8,128)S(1)} fusion(s32[12,512]{1,0:T(8,128)S(1)} %eq.15, f32[16,4,25]{2,1,0:T(4,128)} %param.24), kind=kOutput, calls=%fused_computation.14 | convolution fusion | flops 118063104 | bytes 2488576 | tf_op jit(solution)/shard_map/kbt,krw->btrw/dot_general | solution.py:133
  28.3 1.9 %fusion.169 = (f32[4,1,8,512]{3,1,0,2:T(1,128)S(1)}, f32[4,1,8,512]{3,1,0,2:T(1,128)S(1)}, f32[4,1,8,512]{3,1,0,2:T(1,128)S(1)}, f32[4,1,8,512]{3,1,0,2:T(1,128)...) fusion(f32[4,25,12,512]{3,1,0,2:T(8,128)S(1)} %convolution_bitc, ...), kind=kLoop, calls=%fused_computation.448 | loop fusion | bytes 2490368 | tf_op jit(solution)/shard_map/slice | solution.py:87
  31.1 1.3 fusion.168
  32.4 2.4 %fusion.167 = (f32[4,1,12,512]{3,1,0,2:T(1,128)S(1)}, f32[4,1,12,512]{3,1,0,2:T(1,128)S(1)}, f32[4,1,12,512]{3,1,0,2:T(1,128)}, f32[4,1,12,512]{3,1,0,2:T(1,128)...) fusion(f32[4,25,12,512]{3,1,0,2:T(8,128)S(1)} %convolution_bitc, ...), kind=kLoop, calls=%fused_computation.446 | loop fusion | bytes 3735552 | tf_op jit(solution)/shard_map/slice | solution.py:98
  37.5 1.8 %slice_multiply_fusion.21 = (f32[1,4,8,512]{3,2,1,0:T(8,128)}, f32[1,4,8,512]{3,2,1,0:T(8,128)}) fusion(f32[2,4,8,512]{3,2,1,0:T(8,128)S(1)} %copy-done.41, f32[]{:T(128)} %bitcast.85, f32[]{:T(128)} %bitcast.115), kind=kLoop, calls=%fused_computation.395 | loop fusion | flops 32768 | bytes 262152 | tf_op jit(solution)/shard_map/mul | solution.py:152
  44.9 4.0 %concatenate.73 = bf16[36,4096]{1,0:T(8,128)(2,1)S(1)} concatenate(bf16[4,4096]{1,0:T(4,128)(2,1)} %bitcast.452, bf16[4,4096]{1,0:T(4,128)(2,1)} %bitcast.436, bf16[4,4096]{1,0:T(4,128)(2,1)} %bitcast.448, bf16[4,4096]{1,0:T(4,128)(2,1)} %bitcast.449, bf16[4,4096]{1,0:T(4,128)(2,1)} %bitcast.439, bf16[4,4096]{1,0:T(4,128)(2,1)} %bitcast.450, bf16[4,4096]{1,0:T(4,128)(2,1)} %bitcast.451, ...), dimensions={0} | concatenate | bytes 589824 | tf_op jit(solution)/shard_map/concatenate | solution.py:43
  51.4 1.9 %collective-permute-start.2 = (bf16[128,1,512]{0,2,1:T(8,128)(2,1)S(1)}, bf16[128,1,512]{0,2,1:T(8,128)(2,1)S(1)}, u32[]{:S(2)}, u32[]{:S(2)}) collective-permute-start(bf16[128,1,512]{0,2,1:T(8,128)(2,1)S(1)} %get-tuple-element.131), channel_id=1, source_target_pairs={{0,1},{1,2},{2,3},{3,4},{4,5},{5,6},{6,7},{7,8},{8,9},{9,10},{10,1... | collective-permute-start | bytes 393224 | tf_op jit(solution)/shard_map/ppermute | solution.py:18
  54.4 2.1 %collective-permute-start.6 = (bf16[4,2,512]{2,0,1:T(4,128)(2,1)S(1)}, bf16[4,2,512]{2,0,1:T(4,128)(2,1)S(1)}, u32[]{:S(2)}, u32[]{:S(2)}) collective-permute-start(bf16[4,2,512]{2,0,1:T(4,128)(2,1)S(1)} %get-tuple-element.225), channel_id=1, source_target_pairs={{0,1},{1,2},{2,3},{3,4},{4,5},{5,6},{6,7},{7,8},{8,9},{9,10},{10,1... | collective-permute-start | bytes 24584 | tf_op jit(solution)/shard_map/ppermute | solution.py:18
  56.4 8.5 %collective-permute-start.7 = (bf16[4,2,512]{2,0,1:T(4,128)(2,1)S(1)}, bf16[4,2,512]{2,0,1:T(4,128)(2,1)S(1)}, u32[]{:S(2)}, u32[]{:S(2)}) collective-permute-start(bf16[4,2,512]{2,0,1:T(4,128)(2,1)S(1)} %get-tuple-element.226), channel_id=1, source_target_pairs={{1,0},{2,1},{3,2},{4,3},{5,4},{6,5},{7,6},{8,7},{9,8},{10,9},{11,1... | collective-permute-start | bytes 24584 | tf_op jit(solution)/shard_map/ppermute | solution.py:20
  65.8 2.1 %collective-permute-start.14 = (bf16[4,2,512]{2,0,1:T(4,128)(2,1)S(1)}, bf16[4,2,512]{2,0,1:T(4,128)(2,1)S(1)}, u32[]{:S(2)}, u32[]{:S(2)}) collective-permute-start(bf16[4,2,512]{2,0,1:T(4,128)(2,1)S(1)} %get-tuple-element.231), channel_id=1, source_target_pairs={{0,1},{1,2},{2,3},{3,4},{4,5},{5,6},{6,7},{7,8},{8,9},{9,10},{10,1... | collective-permute-start | bytes 24584 | tf_op jit(solution)/shard_map/ppermute | solution.py:18
  67.8 8.5 %collective-permute-start.15 = (bf16[4,2,512]{2,0,1:T(4,128)(2,1)S(1)}, bf16[4,2,512]{2,0,1:T(4,128)(2,1)S(1)}, u32[]{:S(2)}, u32[]{:S(2)}) collective-permute-start(bf16[4,2,512]{2,0,1:T(4,128)(2,1)S(1)} %get-tuple-element.232), channel_id=1, source_target_pairs={{1,0},{2,1},{3,2},{4,3},{5,4},{6,5},{7,6},{8,7},{9,8},{10,9},{11,1... | collective-permute-start | bytes 24584 | tf_op jit(solution)/shard_map/ppermute | solution.py:20
  76.4 2.1 %collective-permute-start.3 = (bf16[128,1,512]{0,2,1:T(8,128)(2,1)S(1)}, bf16[128,1,512]{0,2,1:T(8,128)(2,1)S(1)}, u32[]{:S(2)}, u32[]{:S(2)}) collective-permute-start(bf16[128,1,512]{0,2,1:T(8,128)(2,1)S(1)} %get-tuple-element.132), channel_id=1, source_target_pairs={{1,0},{2,1},{3,2},{4,3},{5,4},{6,5},{7,6},{8,7},{9,8},{10,9},{11,1... | collective-permute-start | bytes 393224 | tf_op jit(solution)/shard_map/ppermute | solution.py:20
  78.4 4.3 %collective-permute-start.10 = (bf16[128,1,512]{0,2,1:T(8,128)(2,1)S(1)}, bf16[128,1,512]{0,2,1:T(8,128)(2,1)S(1)}, u32[]{:S(2)}, u32[]{:S(2)}) collective-permute-start(bf16[128,1,512]{0,2,1:T(8,128)(2,1)S(1)} %get-tuple-element.137), channel_id=1, source_target_pairs={{0,1},{1,2},{2,3},{3,4},{4,5},{5,6},{6,7},{7,8},{8,9},{9,10},{10,1... | collective-permute-start | bytes 393224 | tf_op jit(solution)/shard_map/ppermute | solution.py:18
  82.7 6.3 %collective-permute-start.11 = (bf16[128,1,512]{0,2,1:T(8,128)(2,1)S(1)}, bf16[128,1,512]{0,2,1:T(8,128)(2,1)S(1)}, u32[]{:S(2)}, u32[]{:S(2)}) collective-permute-start(bf16[128,1,512]{0,2,1:T(8,128)(2,1)S(1)} %get-tuple-element.138), channel_id=1, source_target_pairs={{1,0},{2,1},{3,2},{4,3},{5,4},{6,5},{7,6},{8,7},{9,8},{10,9},{11,1... | collective-permute-start | bytes 393224 | tf_op jit(solution)/shard_map/ppermute | solution.py:20
  97.1 1.3 fusion.173
  101.3 2.6 %fusion.187 = f32[4096,128]{1,0:T(8,128)S(1)} fusion(bf16[1152,4096]{0,1:T(8,128)(2,1)S(1)} %constant_dynamic-update-slice_fusion, bf16[128,1152]{0,1:T(8,128)(2,1)S(1)} %bitcast.431), kind=kOutput, calls=%fused_computation.466 | convolution fusion | flops 1207959552 | bytes 11829248 | tf_op jit(solution)/shard_map/dot_general | solution.py:53
  104.6 1.9 %collective-permute-start.4 = (bf16[128,1,512]{0,2,1:T(8,128)(2,1)S(1)}, bf16[128,1,512]{0,2,1:T(8,128)(2,1)S(1)}, u32[]{:S(2)}, u32[]{:S(2)}) collective-permute-start(bf16[128,1,512]{0,2,1:T(8,128)(2,1)S(1)} %get-tuple-element.127), channel_id=1, source_target_pairs={{0,1},{1,2},{2,3},{3,4},{4,5},{5,6},{6,7},{7,8},{8,9},{9,10},{10,1... | collective-permute-start | bytes 393224 | tf_op jit(solution)/shard_map/ppermute | solution.py:18
  106.5 8.7 %collective-permute-start.5 = (bf16[128,1,512]{0,2,1:T(8,128)(2,1)S(1)}, bf16[128,1,512]{0,2,1:T(8,128)(2,1)S(1)}, u32[]{:S(2)}, u32[]{:S(2)}) collective-permute-start(bf16[128,1,512]{0,2,1:T(8,128)(2,1)S(1)} %get-tuple-element.128), channel_id=1, source_target_pairs={{1,0},{2,1},{3,2},{4,3},{5,4},{6,5},{7,6},{8,7},{9,8},{10,9},{11,1... | collective-permute-start | bytes 393224 | tf_op jit(solution)/shard_map/ppermute | solution.py:20
  115.6 1.3 fusion.174
  119.8 2.6 %fusion.189 = f32[4096,128]{1,0:T(8,128)S(1)} fusion(bf16[1152,4096]{0,1:T(8,128)(2,1)S(1)} %constant_dynamic-update-slice_fusion.8, bf16[128,1152]{0,1:T(8,128)(2,1)S(1)} %bitcast.432), kind=kOutput, calls=%fused_computation.468 | convolution fusion | flops 1207959552 | bytes 11829248 | tf_op jit(solution)/shard_map/dot_general | solution.py:53
  123.7 1.9 %collective-permute-start.12 = (bf16[128,1,512]{0,2,1:T(8,128)(2,1)}, bf16[128,1,512]{0,2,1:T(8,128)(2,1)S(1)}, u32[]{:S(2)}, u32[]{:S(2)}) collective-permute-start(bf16[128,1,512]{0,2,1:T(8,128)(2,1)} %get-tuple-element.133), channel_id=1, source_target_pairs={{0,1},{1,2},{2,3},{3,4},{4,5},{5,6},{6,7},{7,8},{8,9},{9,10},{10,1... | collective-permute-start | bytes 393224 | tf_op jit(solution)/shard_map/ppermute | solution.py:18
  125.6 8.7 %collective-permute-start.13 = (bf16[128,1,512]{0,2,1:T(8,128)(2,1)}, bf16[128,1,512]{0,2,1:T(8,128)(2,1)S(1)}, u32[]{:S(2)}, u32[]{:S(2)}) collective-permute-start(bf16[128,1,512]{0,2,1:T(8,128)(2,1)} %get-tuple-element.134), channel_id=1, source_target_pairs={{1,0},{2,1},{3,2},{4,3},{5,4},{6,5},{7,6},{8,7},{9,8},{10,9},{11,1... | collective-permute-start | bytes 393224 | tf_op jit(solution)/shard_map/ppermute | solution.py:20
  134.7 1.4 reshape.186
  136.1 2.2 %convolution_bitcast_fusion.1 = f32[36,5140]{1,0:T(8,128)S(1)} fusion(bf16[128,5140]{0,1:T(8,128)(2,1)} %reshape.186, bf16[36,128]{1,0:T(8,128)(2,1)S(1)} %reshape.187), kind=kOutput, calls=%fused_computation.2 | convolution fusion | flops 47370240 | bytes 2065216 | tf_op jit(solution)/shard_map/dot_general | solution.py:64
  138.3 1.7 %reshape.188 = f32[9,4,10,514]{3,2,1,0:T(8,128)} reshape(f32[36,5140]{1,0:T(8,128)S(1)} %convolution_bitcast_fusion.1) | data formatting | bytes 1480320 | tf_op jit(solution)/shard_map/reshape | solution.py:69
  140.0 2.2 %fusion.171 = (f32[1,4,8,512]{3,2,1,0:T(8,128)}, f32[1,4,8,512]{3,2,1,0:T(8,128)}, f32[1,4,8,512]{3,2,1,0:T(8,128)}, f32[1,4,8,512]{3,2,1,0:T(8,128)}, f32[1,4,8...) fusion(f32[9,4,10,514]{3,2,1,0:T(8,128)} %reshape.188), kind=kLoop, calls=%fused_computation.450 | loop fusion | bytes 1179648 | tf_op jit(solution)/shard_map/slice | solution.py:74
  144.9 4.8 %fusion.155 = (f32[4,8,512]{2,0,1:T(4,128)S(1)}, f32[4,8,512]{2,0,1:T(4,128)S(1)}) fusion(f32[4,12,512]{2,0,1:T(4,128)} %get-tuple-element.194, f32[4,12,512]{2,0,1:T(4,128)} %get-tuple-element.201, f32[4,12,512]{2,0,1:T(4,128)} %get-tuple-element.200, f32[1,4,8,512]{3,2,1,0:T(8,128)} %get-tuple-element.142, f32[4,12,512]{2,0,1:T(4,128)S(1)} %fusion.164, ...), kind=kLoop, calls=%fused_computation.325 | loop fusion | flops 1327104 | bytes 6357000 | tf_op jit(solution)/shard_map/add | solution.py:153
  149.7 9.9 %all-gather = f32[16,8,512]{2,1,0:T(8,128)S(1)} all-gather(f32[4,8,512]{2,1,0:T(8,128)S(1)} %copy.233), channel_id=2, replica_groups=mesh['tm'=4,'space'=64] {'tm'}, dimensions={0}, use_global_device_ids=true | all-gather | bytes 327680 | tf_op jit(solution)/shard_map/all_gather | solution.py:29
  (212 shorter events, 35.4 us)
Async XLA Ops:
  1.7 39.8 %collective-permute-start = (bf16[4,2,512]{2,0,1:T(4,128)(2,1)S(1)}, bf16[4,2,512]{2,0,1:T(4,128)(2,1)S(1)}, u32[]{:S(2)}, u32[]{:S(2)}) collective-permute-start(bf16[4,2,512]{2,0,1:T(4,128)(2,1)S(1)} %get-tuple-element.227), channel_id=1, source_target_pairs={{0,1},{1,2},{2,3},{3,4},{4,5},{5,6},{6,7},{7,8},{8,9},{9,10},{10,1... | collective-permute-start | bytes 24584 | tf_op jit(solution)/shard_map/ppermute | solution.py:18
  6.6 34.9 %collective-permute-start.1 = (bf16[4,2,512]{2,0,1:T(4,128)(2,1)S(1)}, bf16[4,2,512]{2,0,1:T(4,128)(2,1)S(1)}, u32[]{:S(2)}, u32[]{:S(2)}) collective-permute-start(bf16[4,2,512]{2,0,1:T(4,128)(2,1)S(1)} %get-tuple-element.228), channel_id=1, source_target_pairs={{1,0},{2,1},{3,2},{4,3},{5,4},{6,5},{7,6},{8,7},{9,8},{10,9},{11,1... | collective-permute-start | bytes 24584 | tf_op jit(solution)/shard_map/ppermute | solution.py:20
  14.3 27.4 %collective-permute-start.8 = (bf16[4,2,512]{2,0,1:T(4,128)(2,1)S(1)}, bf16[4,2,512]{2,0,1:T(4,128)(2,1)S(1)}, u32[]{:S(2)}, u32[]{:S(2)}) collective-permute-start(bf16[4,2,512]{2,0,1:T(4,128)(2,1)S(1)} %get-tuple-element.233), channel_id=1, source_target_pairs={{0,1},{1,2},{2,3},{3,4},{4,5},{5,6},{6,7},{7,8},{8,9},{9,10},{10,1... | collective-permute-start | bytes 24584 | tf_op jit(solution)/shard_map/ppermute | solution.py:18
  16.2 25.5 %collective-permute-start.9 = (bf16[4,2,512]{2,0,1:T(4,128)(2,1)S(1)}, bf16[4,2,512]{2,0,1:T(4,128)(2,1)S(1)}, u32[]{:S(2)}, u32[]{:S(2)}) collective-permute-start(bf16[4,2,512]{2,0,1:T(4,128)(2,1)S(1)} %get-tuple-element.234), channel_id=1, source_target_pairs={{1,0},{2,1},{3,2},{4,3},{5,4},{6,5},{7,6},{8,7},{9,8},{10,9},{11,1... | collective-permute-start | bytes 24584 | tf_op jit(solution)/shard_map/ppermute | solution.py:20
  32.4 8.3 %copy-start.48 = (bf16[9,4,128]{2,1,0:T(4,128)(2,1)S(1)}, bf16[9,4,128]{2,1,0:T(4,128)(2,1)}, u32[]{:S(2)}) copy-start(bf16[9,4,128]{2,1,0:T(4,128)(2,1)} %param.23) | copy-start | bytes 27652
  51.4 45.3 %collective-permute-start.2 = (bf16[128,1,512]{0,2,1:T(8,128)(2,1)S(1)}, bf16[128,1,512]{0,2,1:T(8,128)(2,1)S(1)}, u32[]{:S(2)}, u32[]{:S(2)}) collective-permute-start(bf16[128,1,512]{0,2,1:T(8,128)(2,1)S(1)} %get-tuple-element.131), channel_id=1, source_target_pairs={{0,1},{1,2},{2,3},{3,4},{4,5},{5,6},{6,7},{7,8},{8,9},{9,10},{10,1... | collective-permute-start | bytes 393224 | tf_op jit(solution)/shard_map/ppermute | solution.py:18
  53.5 35.6 %copy-start.20 = (f32[4,1,12,512]{3,1,0,2:T(1,128)S(1)}, f32[4,1,12,512]{3,1,0,2:T(1,128)}, u32[]{:S(2)}) copy-start(f32[4,1,12,512]{3,1,0,2:T(1,128)} %get-tuple-element.66) | copy-start | bytes 294916
  53.5 35.6 %copy-start.21 = (f32[4,1,12,512]{3,1,0,2:T(1,128)S(1)}, f32[4,1,12,512]{3,1,0,2:T(1,128)}, u32[]{:S(2)}) copy-start(f32[4,1,12,512]{3,1,0,2:T(1,128)} %get-tuple-element.69) | copy-start | bytes 294916
  54.3 34.9 %copy-start.18 = (f32[4,1,12,512]{3,1,0,2:T(1,128)S(1)}, f32[4,1,12,512]{3,1,0,2:T(1,128)}, u32[]{:S(2)}) copy-start(f32[4,1,12,512]{3,1,0,2:T(1,128)} %get-tuple-element.67) | copy-start | bytes 294916
  54.3 34.9 %copy-start.19 = (f32[4,1,12,512]{3,1,0,2:T(1,128)S(1)}, f32[4,1,12,512]{3,1,0,2:T(1,128)}, u32[]{:S(2)}) copy-start(f32[4,1,12,512]{3,1,0,2:T(1,128)} %get-tuple-element.68) | copy-start | bytes 294916
  54.3 35.6 %copy-start.37 = (f32[4,1,12,512]{3,1,0,2:T(1,128)S(1)}, f32[4,1,12,512]{3,1,0,2:T(1,128)}, u32[]{:S(2)}) copy-start(f32[4,1,12,512]{3,1,0,2:T(1,128)} %get-tuple-element.64) | copy-start | bytes 294916
  54.3 35.6 %copy-start.38 = (f32[4,1,12,512]{3,1,0,2:T(1,128)S(1)}, f32[4,1,12,512]{3,1,0,2:T(1,128)}, u32[]{:S(2)}) copy-start(f32[4,1,12,512]{3,1,0,2:T(1,128)} %get-tuple-element.65) | copy-start | bytes 294916
  54.4 22.0 %collective-permute-start.6 = (bf16[4,2,512]{2,0,1:T(4,128)(2,1)S(1)}, bf16[4,2,512]{2,0,1:T(4,128)(2,1)S(1)}, u32[]{:S(2)}, u32[]{:S(2)}) collective-permute-start(bf16[4,2,512]{2,0,1:T(4,128)(2,1)S(1)} %get-tuple-element.225), channel_id=1, source_target_pairs={{0,1},{1,2},{2,3},{3,4},{4,5},{5,6},{6,7},{7,8},{8,9},{9,10},{10,1... | collective-permute-start | bytes 24584 | tf_op jit(solution)/shard_map/ppermute | solution.py:18
  56.4 22.0 %collective-permute-start.7 = (bf16[4,2,512]{2,0,1:T(4,128)(2,1)S(1)}, bf16[4,2,512]{2,0,1:T(4,128)(2,1)S(1)}, u32[]{:S(2)}, u32[]{:S(2)}) collective-permute-start(bf16[4,2,512]{2,0,1:T(4,128)(2,1)S(1)} %get-tuple-element.226), channel_id=1, source_target_pairs={{1,0},{2,1},{3,2},{4,3},{5,4},{6,5},{7,6},{8,7},{9,8},{10,9},{11,1... | collective-permute-start | bytes 24584 | tf_op jit(solution)/shard_map/ppermute | solution.py:20
  64.9 25.9 %copy-start.35 = (f32[4,1,12,512]{3,1,0,2:T(1,128)S(1)}, f32[4,1,12,512]{3,1,0,2:T(1,128)}, u32[]{:S(2)}) copy-start(f32[4,1,12,512]{3,1,0,2:T(1,128)} %get-tuple-element.61) | copy-start | bytes 294916
  64.9 25.9 %copy-start.36 = (f32[4,1,12,512]{3,1,0,2:T(1,128)S(1)}, f32[4,1,12,512]{3,1,0,2:T(1,128)}, u32[]{:S(2)}) copy-start(f32[4,1,12,512]{3,1,0,2:T(1,128)} %get-tuple-element.62) | copy-start | bytes 294916
  65.7 25.9 %copy-start.33 = (f32[4,1,12,512]{3,1,0,2:T(1,128)S(1)}, f32[4,1,12,512]{3,1,0,2:T(1,128)}, u32[]{:S(2)}) copy-start(f32[4,1,12,512]{3,1,0,2:T(1,128)} %get-tuple-element.59) | copy-start | bytes 294916
  65.7 25.9 %copy-start.34 = (f32[4,1,12,512]{3,1,0,2:T(1,128)S(1)}, f32[4,1,12,512]{3,1,0,2:T(1,128)}, u32[]{:S(2)}) copy-start(f32[4,1,12,512]{3,1,0,2:T(1,128)} %get-tuple-element.60) | copy-start | bytes 294916
  65.7 26.7 %copy-start.31 = (f32[4,1,12,512]{3,1,0,2:T(1,128)S(1)}, f32[4,1,12,512]{3,1,0,2:T(1,128)}, u32[]{:S(2)}) copy-start(f32[4,1,12,512]{3,1,0,2:T(1,128)} %get-tuple-element.56) | copy-start | bytes 294916
  65.7 26.7 %copy-start.32 = (f32[4,1,12,512]{3,1,0,2:T(1,128)S(1)}, f32[4,1,12,512]{3,1,0,2:T(1,128)}, u32[]{:S(2)}) copy-start(f32[4,1,12,512]{3,1,0,2:T(1,128)} %get-tuple-element.57) | copy-start | bytes 294916
  65.8 16.9 %collective-permute-start.14 = (bf16[4,2,512]{2,0,1:T(4,128)(2,1)S(1)}, bf16[4,2,512]{2,0,1:T(4,128)(2,1)S(1)}, u32[]{:S(2)}, u32[]{:S(2)}) collective-permute-start(bf16[4,2,512]{2,0,1:T(4,128)(2,1)S(1)} %get-tuple-element.231), channel_id=1, source_target_pairs={{0,1},{1,2},{2,3},{3,4},{4,5},{5,6},{6,7},{7,8},{8,9},{9,10},{10,1... | collective-permute-start | bytes 24584 | tf_op jit(solution)/shard_map/ppermute | solution.py:18
  67.8 21.2 %collective-permute-start.15 = (bf16[4,2,512]{2,0,1:T(4,128)(2,1)S(1)}, bf16[4,2,512]{2,0,1:T(4,128)(2,1)S(1)}, u32[]{:S(2)}, u32[]{:S(2)}) collective-permute-start(bf16[4,2,512]{2,0,1:T(4,128)(2,1)S(1)} %get-tuple-element.232), channel_id=1, source_target_pairs={{1,0},{2,1},{3,2},{4,3},{5,4},{6,5},{7,6},{8,7},{9,8},{10,9},{11,1... | collective-permute-start | bytes 24584 | tf_op jit(solution)/shard_map/ppermute | solution.py:20
  76.3 16.9 %copy-start.29 = (f32[4,1,12,512]{3,1,0,2:T(1,128)S(1)}, f32[4,1,12,512]{3,1,0,2:T(1,128)}, u32[]{:S(2)}) copy-start(f32[4,1,12,512]{3,1,0,2:T(1,128)} %get-tuple-element.54) | copy-start | bytes 294916
  76.3 16.9 %copy-start.30 = (f32[4,1,12,512]{3,1,0,2:T(1,128)S(1)}, f32[4,1,12,512]{3,1,0,2:T(1,128)}, u32[]{:S(2)}) copy-start(f32[4,1,12,512]{3,1,0,2:T(1,128)} %get-tuple-element.55) | copy-start | bytes 294916
  76.4 20.3 %collective-permute-start.3 = (bf16[128,1,512]{0,2,1:T(8,128)(2,1)S(1)}, bf16[128,1,512]{0,2,1:T(8,128)(2,1)S(1)}, u32[]{:S(2)}, u32[]{:S(2)}) collective-permute-start(bf16[128,1,512]{0,2,1:T(8,128)(2,1)S(1)} %get-tuple-element.132), channel_id=1, source_target_pairs={{1,0},{2,1},{3,2},{4,3},{5,4},{6,5},{7,6},{8,7},{9,8},{10,9},{11,1... | collective-permute-start | bytes 393224 | tf_op jit(solution)/shard_map/ppermute | solution.py:20
  78.4 36.8 %collective-permute-start.10 = (bf16[128,1,512]{0,2,1:T(8,128)(2,1)S(1)}, bf16[128,1,512]{0,2,1:T(8,128)(2,1)S(1)}, u32[]{:S(2)}, u32[]{:S(2)}) collective-permute-start(bf16[128,1,512]{0,2,1:T(8,128)(2,1)S(1)} %get-tuple-element.137), channel_id=1, source_target_pairs={{0,1},{1,2},{2,3},{3,4},{4,5},{5,6},{6,7},{7,8},{8,9},{9,10},{10,1... | collective-permute-start | bytes 393224 | tf_op jit(solution)/shard_map/ppermute | solution.py:18
  82.7 32.5 %collective-permute-start.11 = (bf16[128,1,512]{0,2,1:T(8,128)(2,1)S(1)}, bf16[128,1,512]{0,2,1:T(8,128)(2,1)S(1)}, u32[]{:S(2)}, u32[]{:S(2)}) collective-permute-start(bf16[128,1,512]{0,2,1:T(8,128)(2,1)S(1)} %get-tuple-element.138), channel_id=1, source_target_pairs={{1,0},{2,1},{3,2},{4,3},{5,4},{6,5},{7,6},{8,7},{9,8},{10,9},{11,1... | collective-permute-start | bytes 393224 | tf_op jit(solution)/shard_map/ppermute | solution.py:20
  104.6 29.8 %collective-permute-start.4 = (bf16[128,1,512]{0,2,1:T(8,128)(2,1)S(1)}, bf16[128,1,512]{0,2,1:T(8,128)(2,1)S(1)}, u32[]{:S(2)}, u32[]{:S(2)}) collective-permute-start(bf16[128,1,512]{0,2,1:T(8,128)(2,1)S(1)} %get-tuple-element.127), channel_id=1, source_target_pairs={{0,1},{1,2},{2,3},{3,4},{4,5},{5,6},{6,7},{7,8},{8,9},{9,10},{10,1... | collective-permute-start | bytes 393224 | tf_op jit(solution)/shard_map/ppermute | solution.py:18
  106.5 27.9 %collective-permute-start.5 = (bf16[128,1,512]{0,2,1:T(8,128)(2,1)S(1)}, bf16[128,1,512]{0,2,1:T(8,128)(2,1)S(1)}, u32[]{:S(2)}, u32[]{:S(2)}) collective-permute-start(bf16[128,1,512]{0,2,1:T(8,128)(2,1)S(1)} %get-tuple-element.128), channel_id=1, source_target_pairs={{1,0},{2,1},{3,2},{4,3},{5,4},{6,5},{7,6},{8,7},{9,8},{10,9},{11,1... | collective-permute-start | bytes 393224 | tf_op jit(solution)/shard_map/ppermute | solution.py:20
  123.7 18.6 %collective-permute-start.12 = (bf16[128,1,512]{0,2,1:T(8,128)(2,1)}, bf16[128,1,512]{0,2,1:T(8,128)(2,1)S(1)}, u32[]{:S(2)}, u32[]{:S(2)}) collective-permute-start(bf16[128,1,512]{0,2,1:T(8,128)(2,1)} %get-tuple-element.133), channel_id=1, source_target_pairs={{0,1},{1,2},{2,3},{3,4},{4,5},{5,6},{6,7},{7,8},{8,9},{9,10},{10,1... | collective-permute-start | bytes 393224 | tf_op jit(solution)/shard_map/ppermute | solution.py:18
  125.6 16.7 %collective-permute-start.13 = (bf16[128,1,512]{0,2,1:T(8,128)(2,1)}, bf16[128,1,512]{0,2,1:T(8,128)(2,1)S(1)}, u32[]{:S(2)}, u32[]{:S(2)}) collective-permute-start(bf16[128,1,512]{0,2,1:T(8,128)(2,1)} %get-tuple-element.134), channel_id=1, source_target_pairs={{1,0},{2,1},{3,2},{4,3},{5,4},{6,5},{7,6},{8,7},{9,8},{10,9},{11,1... | collective-permute-start | bytes 393224 | tf_op jit(solution)/shard_map/ppermute | solution.py:20
  144.9 14.8 %copy-start.42 = (f32[4,8,512]{2,1,0:T(8,128)S(1)}, f32[4,8,512]{2,1,0:T(8,128)}, u32[]{:S(2)}) copy-start(f32[4,8,512]{2,1,0:T(8,128)} %param.19) | copy-start | bytes 196612
  (38 other events, 130.8 us)
where the time goes:
time: 162 us; the launch traced here: 161 us
  starting transfers between devices  79.9 us (49%)
  local copies, waits for them, and re-layouts  34.2 us (21%)
  other arithmetic  22 us (14%)
  matrix products  13.2 us (8%)
  blocking collectives  9.94 us (6%)
    ppermute x8, starting transfers between devices, with_halo(): lax.ppermute(head, axis, [((i + 1) % count, i) for i in range(ends)])  58.9 us
    ppermute x8, starting transfers between devices, with_halo(): lax.ppermute(tail, axis, [(i, (i + 1) % count) for i in range(ends)])  20.9 us
    all_gather x1, blocking collectives, entering(): gathered = lax.all_gather(part, axis)  9.94 us
    dot_general x4, matrix products, conv_stacked_in(): total = jnp.dot(flat_kernel, windows, preferred_element_type=jnp.float32)  7.66 us
    mul x10, other arithmetic, blur_adjoint(): padded = jnp.pad(weights[:, tap] * misfit_ext, ((0, 0), (0, 0), (2, 2)))  7.4 us
    unnamed x125, local copies, waits for them, and re-layouts  5.75 us
    add x1, other arithmetic, per_device(): running = running + drift  4.78 us
    concatenate x4, local copies, waits for them, and re-layouts, conv_stacked_in(): jnp.concatenate([padded[:, tap // 3:tap // 3 + out_rows, tap % 3:tap % 3...  4.76 us
  transfers between devices with their start and end apart: 16, of which 0 were waited for; matrix products, arithmetic and copies ran while one was open for 31% of the time, Pallas kernels for 0%

commit v1 on v0

v1 whole, which is shorter than its diff:
```python
import jax
import jax.numpy as jnp
from jax import lax
from jax.experimental import pallas as pl
from jax.experimental.pallas import tpu as pltpu
from jax.sharding import PartitionSpec as P

F32 = jnp.float32
BF16 = jnp.bfloat16
B = 4
R = 8
W = 512
C = 128
TH = 2
HALO = 4
OH = 2
PACK = TH * B * HALO + B * OH
GRP = 16
STR = W // GRP
NPSF = 16
NT = (((1,), (1,)), ((), ()))


def dot(a, b):
    return jnp.dot(a, b, preferred_element_type=F32)


def dot_nt(a, b):
    return lax.dot_general(a, b, NT, preferred_element_type=F32)


def silu(v):
    half = 0.5 * v
    return half + half * jnp.tanh(half)


def shifted(v, by):
    if by == 0:
        return v
    lane = lax.broadcasted_iota(jnp.int32, v.shape, v.ndim - 1)
    moved = pltpu.roll(v, (-by) % W, v.ndim - 1)
    inside = lane < W - by if by > 0 else lane >= -by
    return jnp.where(inside, moved, 0.0)


def pack_kernel(x_ref, obs_ref, a_ref, b_ref, head, tail):
    odd = lax.rem(lax.axis_index("space"), 2) == 1
    for t in range(TH):
        for b in range(B):
            at = (t * B + b) * HALO
            head[at : at + HALO] = x_ref[t, b, :HALO]
            tail[at : at + HALO] = x_ref[t, b, R - HALO :]
    for b in range(B):
        at = TH * B * HALO + b * OH
        head[at : at + OH] = obs_ref[b, :OH]
        tail[at : at + OH] = obs_ref[b, R - OH :]
    first, last = head[...], tail[...]
    a_ref[...] = jnp.where(odd, first, last).astype(BF16)
    b_ref[...] = jnp.where(odd, last, first).astype(BF16)


def main_kernel(
    x_ref, noise_ref, step_ref, scale_ref, bias_ref, start_ref, obs_ref,
    a_ref, b_ref, win_ref, wmid_ref, wout_ref, psf_ref, map_ref,
    loc_ref, tot_ref,
    xs, xcol, obs, mis, wts, perm, h1, h2, halo,
):
    place = lax.axis_index("space")
    top = place == 0
    bottom = place == lax.axis_size("space") - 1
    odd = lax.rem(place, 2) == 1

    q = lax.broadcasted_iota(jnp.int32, (W, W), 0)
    c = lax.broadcasted_iota(jnp.int32, (W, W), 1)
    perm[...] = jnp.where((q & (GRP - 1)) * STR + (q >> 4) == c, 1.0, 0.0).astype(BF16)

    count = map_ref.shape[0]
    spread = jnp.where(
        lax.broadcasted_iota(jnp.int32, (count, W), 1) // R
        == lax.broadcasted_iota(jnp.int32, (count, W), 0),
        1.0,
        0.0,
    ).astype(BF16)
    psf = psf_ref[...]
    psf_hi = psf.astype(BF16)
    rest = psf - psf_hi.astype(F32)
    psf_mid = rest.astype(BF16)
    psf_lo = (rest - psf_mid.astype(F32)).astype(BF16)
    for n in range(3):
        row = jnp.clip(place + (n - 1), 0, count - 1)
        index = map_ref[pl.ds(row, 1), :].astype(F32).astype(BF16)
        pixel = dot(jnp.broadcast_to(index, (16, count)), spread)
        kind = lax.broadcasted_iota(jnp.int32, (NPSF, W), 0).astype(F32)
        one_hot = jnp.where(pixel[:NPSF] == kind, 1.0, 0.0).astype(BF16)
        wts[n] = dot(psf_hi, one_hot) + dot(psf_mid, one_hot) + dot(psf_lo, one_hot)

    got_a, got_b = a_ref[...].astype(F32), b_ref[...].astype(F32)
    halo[0] = jnp.where(top, 0.0, jnp.where(odd, got_a, got_b))
    halo[1] = jnp.where(bottom, 0.0, jnp.where(odd, got_b, got_a))
    for k in range(TH * B):
        xs[k, 0:HALO] = halo[0, k * HALO : (k + 1) * HALO]
        xs[k, HALO : HALO + R] = x_ref[k // B, k % B]
        xs[k, HALO + R : 2 * HALO + R] = halo[1, k * HALO : (k + 1) * HALO]
        xs[k, 2 * HALO + R :] = jnp.zeros((8, W), F32)
    for b in range(B):
        at = TH * B * HALO + b * OH
        obs[b, 0:OH] = halo[0, at : at + OH]
        obs[b, OH : OH + R] = obs_ref[b]
        obs[b, OH + R : 2 * OH + R] = halo[1, at : at + OH]
        obs[b, 2 * OH + R :] = jnp.zeros((4, W), F32)

    for n, by in enumerate((-2, -1, 0, 1, 2)):
        for k in range(TH * B):
            xcol[n, k] = shifted(xs[k], by)
    sub = lax.broadcasted_iota(jnp.int32, (R, W), 0)
    keep_one = jnp.logical_or(sub >= OH, jnp.logical_not(top))
    keep_two = jnp.logical_or(sub < OH, jnp.logical_not(bottom))
    guidance = [None] * (TH * B)
    for b in range(B):
        one = [jnp.zeros((R, W), F32) for _ in range(TH)]
        two = [jnp.zeros((R, W), F32) for _ in range(TH)]
        for tap in range(25):
            i = tap // 5
            up, own, down = (wts[n, pl.ds(b * 25 + tap, 1), :] for n in range(3))
            w_one = jnp.where(sub < OH, up, own)
            w_two = jnp.where(sub < OH, own, down)
            for t in range(TH):
                one[t] = one[t] + w_one * xcol[tap % 5, t * B + b, i : i + R]
                two[t] = two[t] + w_two * xcol[tap % 5, t * B + b, R + i : 2 * R + i]
        for t in range(TH):
            mis[t * B + b, :R] = jnp.where(keep_one, obs[b, :R] - one[t], 0.0)
            mis[t * B + b, R:] = jnp.where(keep_two, obs[b, R:] - two[t], 0.0)
        total = [jnp.zeros((R, W), F32) for _ in range(TH)]
        for j in range(5):
            part = [jnp.zeros((R, W), F32) for _ in range(TH)]
            for i in range(5):
                off = i - 2
                up, own, down = (wts[n, pl.ds(b * 25 + i * 5 + j, 1), :] for n in range(3))
                if off > 0:
                    w = jnp.where(sub < off, up, own)
                elif off < 0:
                    w = jnp.where(sub >= R + off, down, own)
                else:
                    w = own
                for t in range(TH):
                    part[t] = part[t] + w * mis[t * B + b, OH - off : OH - off + R]
            for t in range(TH):
                total[t] = total[t] + shifted(part[t], 2 - j)
        for t in range(TH):
            guidance[t * B + b] = total[t]

    running = [None] * B
    for t in range(TH):
        flat = xs[t * B : (t + 1) * B, : 2 * R].reshape(B * 2 * R, W)
        taps = jnp.concatenate([shifted(flat, by) for by in (-1, 0, 1)], axis=0).astype(BF16)
        source = dot_nt(perm[...], taps).astype(BF16)
        bias = bias_ref[t : t + 1, :]
        bias = jnp.concatenate([bias, bias], axis=1)
        edge_row = lax.broadcasted_iota(jnp.int32, (GRP, 2 * C), 0)
        for p in range(6):
            hidden = silu(dot(source, win_ref[p]) + bias)
            if p == 0:
                hidden = jnp.where(top, 0.0, hidden)
            if p == 5:
                hidden = jnp.where(bottom, 0.0, hidden)
            h1[p, GRP : GRP + W] = hidden.astype(BF16)
            before = pltpu.roll(hidden[W - GRP :], 1, 0)
            h1[p, :GRP] = jnp.where(edge_row > 0, before, 0.0).astype(BF16)
            after = pltpu.roll(hidden[:GRP], GRP - 1, 0)
            h1[p, GRP + W :] = jnp.where(edge_row < GRP - 1, after, 0.0).astype(BF16)
        lane = lax.broadcasted_iota(jnp.int32, (W, 2 * C), 1)
        for j in range(5):
            windows = jnp.concatenate(
                [h1[j + n, GRP * d : GRP * d + W] for d in range(3) for n in range(2)], axis=1
            )
            kept = jnp.concatenate(
                [h1[j, GRP : GRP + W, C:], h1[j + 1, GRP : GRP + W, :C]], axis=1
            ).astype(F32)
            hidden = kept + silu(dot(windows, wmid_ref[...]))
            if j == 0:
                hidden = jnp.where(jnp.logical_and(top, lane < C), 0.0, hidden)
            if j == 4:
                hidden = jnp.where(jnp.logical_and(bottom, lane >= C), 0.0, hidden)
            h2[:, 2 * C * j : 2 * C * (j + 1)] = hidden.astype(BF16)
        product = dot_nt(wout_ref[...], h2[...])
        high = product.astype(BF16)
        low = (product - high.astype(F32)).astype(BF16)
        product = dot(high, perm[...]) + dot(low, perm[...])
        for b in range(B):
            score = 0.0
            for d in range(3):
                at = (d * B + b) * R
                score = score + shifted(product[at : at + R], d - 1)
            drift = (
                step_ref[t] * (score + guidance[t * B + b]) + scale_ref[t] * noise_ref[t, b]
            )
            running[b] = drift if t == 0 else running[b] + drift
            loc_ref[t, b] = start_ref[b] + running[b]
            if t == TH - 1:
                tot_ref[b] = running[b]


def weights_in(kernel):
    taps = kernel.reshape(3, 3, C, B).transpose(1, 3, 0, 2)
    pairs = []
    for p in range(6):
        subs = []
        for s in range(2):
            lead = 1 + 2 * p + s
            subs.append(jnp.pad(taps, ((0, 0), (0, 0), (lead, 2 * R - 3 - lead), (0, 0))))
        pairs.append(jnp.stack(subs, axis=3).reshape(3 * B * 2 * R, 2 * C))
    return jnp.stack(pairs)


def weights_mid(kernel):
    taps = kernel.reshape(3, 3, C, C).transpose(1, 0, 3, 2)
    subs = [jnp.pad(taps, ((0, 0), (s, 1 - s), (0, 0), (0, 0))) for s in range(2)]
    return jnp.stack(subs, axis=3).reshape(3 * 4 * C, 2 * C)


def weights_out(kernel):
    taps = kernel.reshape(3, 3, B, C).transpose(1, 2, 0, 3)
    rows = [jnp.pad(taps, ((0, 0), (0, 0), (r, 7 - r), (0, 0))) for r in range(R)]
    return jnp.stack(rows, axis=2).reshape(3 * B * R, 10 * C)


def per_device(
    trajectory, noise, step_size, noise_scale, time_bias, start_state, observed,
    conv_in, conv_mid, conv_out, psf_bank, index_map,
):
    vmem = pl.BlockSpec(memory_space=pltpu.VMEM)
    smem = pl.BlockSpec(memory_space=pltpu.SMEM)
    packed = jax.ShapeDtypeStruct((PACK, W), BF16)
    send_a, send_b = pl.pallas_call(
        pack_kernel,
        out_shape=(packed, packed),
        in_specs=[vmem, vmem],
        out_specs=(vmem, vmem),
        scratch_shapes=[pltpu.VMEM((PACK, W), F32)] * 2,
    )(trajectory, observed)

    n = lax.axis_size("space")
    swap_a = [(i, i ^ 1) for i in range(n)]
    swap_b = [(i, i) if i in (0, n - 1) else (i, ((i + 1) ^ 1) - 1) for i in range(n)]
    got_b = lax.ppermute(send_b, "space", swap_b)
    got_a = lax.ppermute(send_a, "space", swap_a)

    psf = psf_bank.reshape(NPSF, 25 * B).T
    psf = jnp.pad(psf, ((0, 4), (0, 0)))
    local = jax.ShapeDtypeStruct((TH, B, R, W), F32)
    total = jax.ShapeDtypeStruct((B, R, W), F32)
    loc, tot = pl.pallas_call(
        main_kernel,
        out_shape=(local, total),
        in_specs=[vmem, vmem, smem, smem] + [vmem] * 10,
        out_specs=(vmem, vmem),
        scratch_shapes=[
            pltpu.VMEM((TH * B, 3 * R, W), F32),
            pltpu.VMEM((5, TH * B, 3 * R, W), F32),
            pltpu.VMEM((B, 2 * R, W), F32),
            pltpu.VMEM((TH * B, 2 * R, W), F32),
            pltpu.VMEM((3, 104, W), F32),
            pltpu.VMEM((W, W), BF16),
            pltpu.VMEM((6, W + 2 * GRP, 2 * C), BF16),
            pltpu.VMEM((W, 10 * C), BF16),
            pltpu.VMEM((2, PACK, W), F32),
        ],
        compiler_params=pltpu.CompilerParams(vmem_limit_bytes=48 * 1024 * 1024),
    )(
        trajectory, noise, step_size, noise_scale, time_bias, start_state, observed,
        got_a, got_b, weights_in(conv_in), weights_mid(conv_mid), weights_out(conv_out),
        psf, index_map,
    )

    m = lax.axis_size("tm")
    me = lax.axis_index("tm")
    before = 0.0
    for k in range(1, m):
        part = lax.ppermute(tot, "tm", [(i, (i + k) % m) for i in range(m)])
        before = before + jnp.where(me >= k, part, 0.0)
    return loc + before


def solution(mesh):
    return jax.shard_map(
        per_device,
        mesh=mesh,
        in_specs=(
            P("tm", None, "space", None),
            P("tm", None, "space", None),
            P("tm"),
            P("tm"),
            P("tm", None),
            P(None, "space", None),
            P(None, "space", None),
            P(),
            P(),
            P(),
            P(),
            P(),
        ),
        out_specs=P("tm", None, "space", None),
        check_vma=False,
    )
```

time: 162 us -> 37.6 us (0.23)
  the two profiles are of different devices: /device:TPU:7 before, /device:TPU:6 now
where the time goes in v1:
time: 37.6 us; the launch traced here: 37.3 us
  starting transfers between devices  13.7 us (36%)
  Pallas kernels  12.7 us (34%)
  local copies, waits for them, and re-layouts  5.24 us (14%)
  waiting for transfers between devices  4.11 us (11%)
  other arithmetic  1.18 us (3%)
    pallas_call x1, Pallas kernels, per_device(): pl.pallas_call(main_kernel, out_shape=(local, total), in_specs=[vmem, vme...  11.1 us
    ppermute x1, starting transfers between devices, per_device(): got_b = lax.ppermute(send_b, 'space', swap_b)  9.09 us
    ppermute x3, waiting for transfers between devices, per_device(): part = lax.ppermute(tot, 'tm', [(i, (i + k) % m) for i in range(m)])  4.1 us
    ppermute x1, starting transfers between devices, per_device(): got_a = lax.ppermute(send_a, 'space', swap_a)  3.27 us
    unnamed x37, local copies, waits for them, and re-layouts  3.01 us
    pallas_call x1, Pallas kernels, per_device(): pl.pallas_call(pack_kernel, out_shape=(packed, packed), in_specs=[vmem, v...  1.6 us
    ppermute x3, starting transfers between devices, per_device(): part = lax.ppermute(tot, 'tm', [(i, (i + k) % m) for i in range(m)])  1.34 us
    another operation x7, local copies, waits for them, and re-layouts, weights_in(): pairs.append(jnp.stack(subs, axis=3).reshape(3 * B * 2 * R, 2 * C))  0.81 us
  transfers between devices with their start and end apart: 5, of which 3 were waited for; matrix products, arithmetic and copies ran while one was open for 8% of the time, Pallas kernels for 0%

profile of v1, /device:TPU:6, one launch (start us, length us, event | category | flops | bytes accessed | tf_op | source)
XLA Modules:
  0.0 37.3 jit_solution(14417736768524954306)
XLA Ops:
  0.0 1.6 %shard_map.118 = (bf16[40,512]{1,0:T(8,128)(2,1)}, bf16[40,512]{1,0:T(8,128)(2,1)}) custom-call(f32[2,4,8,512]{3,2,1,0:T(8,128)} %x_ref.3, f32[4,8,512]{2,1,0:T(8,128)} %obs_ref.3), custom_call_target="tpu_custom_call" | custom-call | tf_op jit(solution)/shard_map/pallas_call | solution.py:234
  1.6 3.3 %collective-permute-start = (bf16[40,512]{1,0:T(8,128)(2,1)}, bf16[40,512]{1,0:T(8,128)(2,1)S(1)}, u32[]{:S(2)}, u32[]{:S(2)}) collective-permute-start(bf16[40,512]{1,0:T(8,128)(2,1)} %get-tuple-element.9), channel_id=1, source_target_pairs={{0,1},{1,0},{2,3},{3,2},{4,5},{5,4},{6,7},{7,6},{8,9},{9,8},{10,11... | collective-permute-start | bytes 122888 | tf_op jit(solution)/shard_map/ppermute | solution.py:246
  4.9 9.1 %collective-permute-start.1 = (bf16[40,512]{1,0:T(8,128)(2,1)}, bf16[40,512]{1,0:T(8,128)(2,1)S(1)}, u32[]{:S(2)}, u32[]{:S(2)}) collective-permute-start(bf16[40,512]{1,0:T(8,128)(2,1)} %get-tuple-element.10), channel_id=1, source_target_pairs={{0,0},{1,2},{2,1},{3,4},{4,3},{5,6},{6,5},{7,8},{8,7},{9,10},{10,9... | collective-permute-start | bytes 122888 | tf_op jit(solution)/shard_map/ppermute | solution.py:245
  14.0 0.2 pad_bitcast_fusion.3
  14.2 0.1 pad_maximum_fusion.1
  14.3 0.1 copy.40
  14.5 0.1 copy.41
  14.7 0.1 pad_maximum_fusion.3
  14.9 0.1 copy.42
  15.0 0.1 copy.43
  15.2 0.1 pad_maximum_fusion.5
  15.4 0.1 copy.44
  15.6 0.1 copy.47
  15.8 0.7 %copy-done.9 = bf16[9,128,128]{2,1,0:T(8,128)(2,1)S(1)} copy-done((bf16[9,128,128]{2,1,0:T(8,128)(2,1)S(1)}, bf16[9,128,128]{2,1,0:T(8,128)(2,1)}, u32[]{:S(2)}) %copy-start.9) | copy-done | bytes 294936
  16.5 0.1 pad_bitcast_fusion.1
  16.6 0.6 %copy-done.8 = bf16[9,4,128]{2,1,0:T(4,128)(2,1)S(1)} copy-done((bf16[9,4,128]{2,1,0:T(4,128)(2,1)S(1)}, bf16[9,4,128]{2,1,0:T(4,128)(2,1)}, u32[]{:S(2)}) %copy-start.8) | copy-done | bytes 9240
  17.4 0.1 pad_maximum_fusion
  17.5 0.6 %copy.50 = bf16[3,4,128,2,128]{4,3,2,1,0:T(2,128)(2,1)S(1)} copy(bf16[3,4,128,2,128]{2,4,0,1,3:T(8,128)(2,1)S(1)} %pad_maximum_fusion) | data formatting | bytes 1572864 | tf_op jit(solution)/shard_map/stack | solution.py:218
  18.1 0.1 copy.60
  18.3 0.7 %copy-done.10 = f32[16,4,25]{2,1,0:T(4,128)S(1)} copy-done((f32[16,4,25]{2,1,0:T(4,128)S(1)}, f32[16,4,25]{2,1,0:T(4,128)}, u32[]{:S(2)}) %copy-start.10) | copy-done | bytes 6424
  19.0 0.1 reshape.24
  19.1 0.1 copy.54
  19.3 0.6 %copy-done = f32[2,4,8,512]{3,2,1,0:T(8,128)S(1)} copy-done((f32[2,4,8,512]{3,2,1,0:T(8,128)S(1)}, f32[2,4,8,512]{3,2,1,0:T(8,128)}, u32[]{:S(2)}) %copy-start) | copy-done | bytes 131096
  19.9 0.1 copy-done.1
  20.0 11.1 %shard_map.119 = (f32[2,4,8,512]{3,2,1,0:T(8,128)S(1)}, f32[4,8,512]{2,1,0:T(8,128)S(1)}) custom-call(f32[2,4,8,512]{3,2,1,0:T(8,128)S(1)} %copy-done, f32[2,4,8,512]{3,2,1,0:T(8,128)S(1)} %copy-done.2, f32[2]{0:T(128)S(1)} %copy-done.6, f32[2]{0:T(128)S(1)} %copy-done.7, f32[2,128]{1,0:T(2,128)S(1)} %copy-done.5, f32[4,8,512]{2,1,0:T(8,128)S(1)} %copy-done.3, ...), custom_call_target="tpu_custom_call" | custom-call | tf_op jit(solution)/shard_map/pallas_call | solution.py:252
  31.2 0.1 collective-permute-start.4
  31.3 1.1 %collective-permute-start.3 = (f32[4,8,512]{2,1,0:T(8,128)S(1)}, f32[4,8,512]{2,1,0:T(8,128)S(1)}, u32[]{:S(2)}, u32[]{:S(2)}) collective-permute-start(f32[4,8,512]{2,1,0:T(8,128)S(1)} %get-tuple-element.12), channel_id=1, source_target_pairs={{0,128},{64,192},{128,0},{192,64},{1,129},{65,193},{129,1},{193,65... | collective-permute-start | bytes 196616 | tf_op jit(solution)/shard_map/ppermute | solution.py:279
  32.4 0.1 collective-permute-start.2
  32.5 0.7 %collective-permute-done.4 = f32[4,8,512]{2,1,0:T(8,128)S(1)} collective-permute-done((f32[4,8,512]{2,1,0:T(8,128)S(1)}, f32[4,8,512]{2,1,0:T(8,128)S(1)}, u32[]{:S(2)}, u32[]{:S(2)}) %collective-permute-start.4) | collective-permute-done | bytes 65568 | tf_op jit(solution)/shard_map/ppermute | solution.py:279
  33.2 3.0 %collective-permute-done.3 = f32[4,8,512]{2,1,0:T(8,128)S(1)} collective-permute-done((f32[4,8,512]{2,1,0:T(8,128)S(1)}, f32[4,8,512]{2,1,0:T(8,128)S(1)}, u32[]{:S(2)}, u32[]{:S(2)}) %collective-permute-start.3) | collective-permute-done | bytes 65568 | tf_op jit(solution)/shard_map/ppermute | solution.py:279
  36.3 0.4 collective-permute-done.2
  36.6 0.7 %broadcast_add_fusion = f32[2,4,8,512]{3,2,1,0:T(8,128)} fusion(f32[2,4,8,512]{3,2,1,0:T(8,128)S(1)} %get-tuple-element.11, f32[4,8,512]{2,1,0:T(8,128)S(1)} %select_add_fusion), kind=kLoop, calls=%fused_computation.10 | loop fusion | flops 32768 | bytes 327680 | tf_op jit(solution)/shard_map/add | solution.py:281
  (44 shorter events, 0.7 us)
Async XLA Ops:
  0.0 14.0 %copy-start.11 = (bf16[9,128,4]{1,2,0:T(4,128)(2,1)S(1)}, bf16[9,128,4]{1,2,0:T(4,128)(2,1)}, u32[]{:S(2)}) copy-start(bf16[9,128,4]{1,2,0:T(4,128)(2,1)} %param.19) | copy-start | bytes 27652
  1.6 17.6 %collective-permute-start = (bf16[40,512]{1,0:T(8,128)(2,1)}, bf16[40,512]{1,0:T(8,128)(2,1)S(1)}, u32[]{:S(2)}, u32[]{:S(2)}) collective-permute-start(bf16[40,512]{1,0:T(8,128)(2,1)} %get-tuple-element.9), channel_id=1, source_target_pairs={{0,1},{1,0},{2,3},{3,2},{4,5},{5,4},{6,7},{7,6},{8,9},{9,8},{10,11... | collective-permute-start | bytes 122888 | tf_op jit(solution)/shard_map/ppermute | solution.py:246
  4.9 14.3 %collective-permute-start.1 = (bf16[40,512]{1,0:T(8,128)(2,1)}, bf16[40,512]{1,0:T(8,128)(2,1)S(1)}, u32[]{:S(2)}, u32[]{:S(2)}) collective-permute-start(bf16[40,512]{1,0:T(8,128)(2,1)} %get-tuple-element.10), channel_id=1, source_target_pairs={{0,0},{1,2},{2,1},{3,4},{4,3},{5,6},{6,5},{7,8},{8,7},{9,10},{10,9... | collective-permute-start | bytes 122888 | tf_op jit(solution)/shard_map/ppermute | solution.py:245
  15.5 1.0 %copy-start.9 = (bf16[9,128,128]{2,1,0:T(8,128)(2,1)S(1)}, bf16[9,128,128]{2,1,0:T(8,128)(2,1)}, u32[]{:S(2)}) copy-start(bf16[9,128,128]{2,1,0:T(8,128)(2,1)} %param.20) | copy-start | bytes 884740
  16.5 0.7 %copy-start.8 = (bf16[9,4,128]{2,1,0:T(4,128)(2,1)S(1)}, bf16[9,4,128]{2,1,0:T(4,128)(2,1)}, u32[]{:S(2)}) copy-start(bf16[9,4,128]{2,1,0:T(4,128)(2,1)} %param.21) | copy-start | bytes 27652
  18.2 0.8 %copy-start.10 = (f32[16,4,25]{2,1,0:T(4,128)S(1)}, f32[16,4,25]{2,1,0:T(4,128)}, u32[]{:S(2)}) copy-start(f32[16,4,25]{2,1,0:T(4,128)} %param.22) | copy-start | bytes 19204
  18.2 1.0 %copy-start.2 = (f32[2,4,8,512]{3,2,1,0:T(8,128)S(1)}, f32[2,4,8,512]{3,2,1,0:T(8,128)}, u32[]{:S(2)}) copy-start(f32[2,4,8,512]{3,2,1,0:T(8,128)} %noise_ref.1) | copy-start | bytes 393220
  18.3 1.0 %copy-start.3 = (f32[4,8,512]{2,1,0:T(8,128)S(1)}, f32[4,8,512]{2,1,0:T(8,128)}, u32[]{:S(2)}) copy-start(f32[4,8,512]{2,1,0:T(8,128)} %start_ref.1) | copy-start | bytes 196612
  18.3 1.0 %copy-start.4 = (s32[64,64]{1,0:T(8,128)S(1)}, s32[64,64]{1,0:T(8,128)}, u32[]{:S(2)}) copy-start(s32[64,64]{1,0:T(8,128)} %map_ref.1) | copy-start | bytes 49156
  19.0 0.9 %copy-start = (f32[2,4,8,512]{3,2,1,0:T(8,128)S(1)}, f32[2,4,8,512]{3,2,1,0:T(8,128)}, u32[]{:S(2)}) copy-start(f32[2,4,8,512]{3,2,1,0:T(8,128)} %x_ref.3) | copy-start | bytes 393220
  19.1 0.8 %copy-start.7 = (f32[2]{0:T(128)S(1)}, f32[2]{0:T(128)}, u32[]{:S(2)}) copy-start(f32[2]{0:T(128)} %scale_ref.1) | copy-start | bytes 28
  19.2 0.9 %copy-start.1 = (f32[4,8,512]{2,1,0:T(8,128)S(1)}, f32[4,8,512]{2,1,0:T(8,128)}, u32[]{:S(2)}) copy-start(f32[4,8,512]{2,1,0:T(8,128)} %obs_ref.3) | copy-start | bytes 196612
  19.2 0.8 %copy-start.5 = (f32[2,128]{1,0:T(2,128)S(1)}, f32[2,128]{1,0:T(2,128)}, u32[]{:S(2)}) copy-start(f32[2,128]{1,0:T(2,128)} %bias_ref.1) | copy-start | bytes 3076
  19.2 0.8 %copy-start.6 = (f32[2]{0:T(128)S(1)}, f32[2]{0:T(128)}, u32[]{:S(2)}) copy-start(f32[2]{0:T(128)} %step_ref.1) | copy-start | bytes 28
  31.2 2.1 %collective-permute-start.4 = (f32[4,8,512]{2,1,0:T(8,128)S(1)}, f32[4,8,512]{2,1,0:T(8,128)S(1)}, u32[]{:S(2)}, u32[]{:S(2)}) collective-permute-start(f32[4,8,512]{2,1,0:T(8,128)S(1)} %get-tuple-element.12), channel_id=1, source_target_pairs={{0,192},{64,0},{128,64},{192,128},{1,193},{65,1},{129,65},{193,129... | collective-permute-start | bytes 196616 | tf_op jit(solution)/shard_map/ppermute | solution.py:279
  31.3 5.0 %collective-permute-start.3 = (f32[4,8,512]{2,1,0:T(8,128)S(1)}, f32[4,8,512]{2,1,0:T(8,128)S(1)}, u32[]{:S(2)}, u32[]{:S(2)}) collective-permute-start(f32[4,8,512]{2,1,0:T(8,128)S(1)} %get-tuple-element.12), channel_id=1, source_target_pairs={{0,128},{64,192},{128,0},{192,64},{1,129},{65,193},{129,1},{193,65... | collective-permute-start | bytes 196616 | tf_op jit(solution)/shard_map/ppermute | solution.py:279
  32.4 4.3 %collective-permute-start.2 = (f32[4,8,512]{2,1,0:T(8,128)S(1)}, f32[4,8,512]{2,1,0:T(8,128)S(1)}, u32[]{:S(2)}, u32[]{:S(2)}) collective-permute-start(f32[4,8,512]{2,1,0:T(8,128)S(1)} %get-tuple-element.12), channel_id=1, source_target_pairs={{0,64},{64,128},{128,192},{192,0},{1,65},{65,129},{129,193},{193,1... | collective-permute-start | bytes 196616 | tf_op jit(solution)/shard_map/ppermute | solution.py:279

commit v2 on v1

v2 whole, which is shorter than its diff:
```python
import jax
import jax.numpy as jnp
from jax import lax
from jax.experimental import pallas as pl
from jax.experimental.pallas import tpu as pltpu
from jax.sharding import PartitionSpec as P

F32 = jnp.float32
BF16 = jnp.bfloat16
B = 4
R = 8
W = 512
C = 128
TH = 2
HALO = 4
OH = 2
PACK = TH * B * HALO + B * OH
LANES = 128
GRP = 16
STR = W // GRP
NPSF = 16
MIB = 1024 * 1024
TAP_ROWS = 3 * B * 2 * R
NT = (((1,), (1,)), ((), ()))


def dot(a, b):
    return jnp.dot(a, b, preferred_element_type=F32)


def dot_nt(a, b):
    return lax.dot_general(a, b, NT, preferred_element_type=F32)


def dot_tn(a, b):
    return lax.dot_general(a, b, (((0,), (0,)), ((), ())), preferred_element_type=F32)


def silu_of_half(half):
    return half + half * jnp.tanh(half)


def shifted(v, by):
    if by == 0:
        return v
    lane = lax.broadcasted_iota(jnp.int32, v.shape, v.ndim - 1)
    moved = pltpu.roll(v, (-by) % W, v.ndim - 1)
    inside = lane < W - by if by > 0 else lane >= -by
    return jnp.where(inside, moved, 0.0)


def pack_kernel(x_hbm, obs_hbm, f_ref, s_ref, b_ref, x, obs, head, tail, sems):
    copies = [
        pltpu.make_async_copy(x_hbm, x, sems.at[0]),
        pltpu.make_async_copy(obs_hbm, obs, sems.at[1]),
    ]
    for copy in copies:
        copy.start()
    second = lax.axis_index("space") == 1
    for copy in copies:
        copy.wait()
    for t in range(TH):
        for b in range(B):
            at = (t * B + b) * HALO
            head[at : at + HALO] = x[t, b, :HALO]
            tail[at : at + HALO] = x[t, b, R - HALO :]
    for b in range(B):
        at = TH * B * HALO + b * OH
        head[at : at + OH] = obs[b, :OH]
        tail[at : at + OH] = obs[b, R - OH :]
    first, last = head[...], tail[...]
    f_ref[...] = jnp.where(second, first, last).astype(BF16)
    rest = jnp.where(second, last, first).astype(BF16)
    s_ref[...] = rest
    b_ref[...] = rest


def tables_kernel(
    psf_ref, map_ref, bias_ref, step_ref, scale_ref, perm_ref, wts_ref, rate_ref, bank
):
    place = lax.axis_index("space")

    count = map_ref.shape[0]
    blocks = [map_ref[pl.ds(jnp.clip(place + n - 1, 0, count - 1), 1), :] for n in range(3)]
    blocks = jnp.concatenate(blocks + [jnp.zeros((13, count), jnp.int32)], axis=0)
    spread = jnp.where(
        (lax.broadcasted_iota(jnp.int32, (count, W), 1) >> 3)
        == lax.broadcasted_iota(jnp.int32, (count, W), 0),
        1.0,
        0.0,
    ).astype(BF16)
    pixel = dot(blocks.astype(F32).astype(BF16), spread)
    kind = lax.broadcasted_iota(jnp.int32, (NPSF, W), 0).astype(F32)
    one_hot = jnp.concatenate(
        [jnp.where(pixel[n : n + 1] == kind, 1.0, 0.0) for n in range(3)], axis=1
    ).astype(BF16)
    bank[...] = jnp.zeros_like(bank)
    for b in range(B):
        bank[:, 32 * b : 32 * b + 25] = psf_ref[:, b, :]
    psf = bank[...]
    high = psf.astype(BF16)
    rest = psf - high.astype(F32)
    mid = rest.astype(BF16)
    low = (rest - mid.astype(F32)).astype(BF16)
    picked = dot_tn(
        jnp.concatenate([high, mid, low], axis=0), jnp.concatenate([one_hot] * 3, axis=0)
    )
    for n in range(3):
        wts_ref[n] = picked[:, n * W : (n + 1) * W]

    q = lax.broadcasted_iota(jnp.int32, (W, 1), 0)
    c = lax.broadcasted_iota(jnp.int32, (W, W), 1)
    perm_ref[...] = jnp.where((q & (GRP - 1)) * STR + (q >> 4) == c, 1.0, 0.0).astype(BF16)

    for t in range(TH):
        rate_ref[t : t + 1, :] = jnp.full((1, W), step_ref[t], F32)
        rate_ref[TH + t : TH + t + 1, :] = jnp.full((1, W), scale_ref[t], F32)
        rate_ref[2 * TH + t : 2 * TH + t + 1, :C] = bias_ref[t : t + 1, :]


def weights_kernel(
    win_raw, wmid_raw, wout_raw, rate_ref, win_ref, wmid_ref, wout_ref, wide, tall
):
    wide[...] = jnp.zeros_like(wide)
    for tap in range(9):
        dy, dx = tap // 3, tap % 3
        rows = 0.5 * win_raw[tap].astype(F32)
        for p in range(6):
            for s in range(2):
                for b in range(B):
                    at = (dx * B + b) * 2 * R + dy + 1 + 2 * p + s
                    wide[p, at : at + 1, s * C : (s + 1) * C] = rows[b : b + 1]
    for t in range(TH):
        rest = 0.5 * rate_ref[2 * TH + t : 2 * TH + t + 1, :C]
        for n in range(3):
            part = rest.astype(BF16).astype(F32)
            rest = rest - part
            at = TAP_ROWS + 3 * t + n
            for p in range(6):
                wide[p, at : at + 1, :C] = part
                wide[p, at : at + 1, C:] = part
    for p in range(6):
        win_ref[p] = wide[p].astype(BF16)

    for dx in range(3):
        for s in range(2):
            at = (dx * 4 + 3 * (1 - s)) * C
            wmid_ref[at : at + C, s * C : (s + 1) * C] = jnp.zeros((C, C), BF16)
        for dy in range(3):
            block = (0.5 * wmid_raw[dy * 3 + dx].astype(F32)).T.astype(BF16)
            for s in range(2):
                at = (dx * 4 + dy + s) * C
                wmid_ref[at : at + C, s * C : (s + 1) * C] = block

    tall[...] = jnp.zeros_like(tall)
    for tap in range(9):
        dy, dx = tap // 3, tap % 3
        rows = wout_raw[tap].astype(F32)
        for b in range(B):
            for r in range(R):
                at = (dx * B + b) * R + r
                tall[at : at + 1, (r + dy) * C : (r + dy + 1) * C] = rows[b : b + 1]
    wout_ref[...] = tall[...].T.astype(BF16)


def main_kernel(
    x_ref, noise_ref, start_ref, obs_ref, f_ref, s_ref, b_ref,
    win_ref, wmid_ref, wout_ref, perm, wts, rate_ref,
    loc_ref, tot_ref,
    xcol, obs, rows, mis, parts, src, h1, h2, halo,
):
    place = lax.axis_index("space")
    top = place == 0
    bottom = place == lax.axis_size("space") - 1

    got_f, got_s, got_b = (ref[...].astype(F32) for ref in (f_ref, s_ref, b_ref))
    halo[0] = jnp.where(top, 0.0, jnp.where(place == 2, got_s, got_f))
    below = jnp.where(top, got_f, jnp.where(place == 1, got_s, got_b))
    halo[1] = jnp.where(bottom, 0.0, below)
    for k in range(TH * B):
        xcol[2, k, 0:HALO] = halo[0, k * HALO : (k + 1) * HALO]
        xcol[2, k, HALO : HALO + R] = x_ref[k // B, k % B]
        xcol[2, k, HALO + R :] = halo[1, k * HALO : (k + 1) * HALO]
        for n in (0, 1, 3, 4):
            xcol[n, k] = shifted(xcol[2, k], n - 2)
    for b in range(B):
        at = TH * B * HALO + b * OH
        obs[b, 0:OH] = halo[0, at : at + OH]
        obs[b, OH : OH + R] = obs_ref[b]
        obs[b, OH + R : 2 * OH + R] = halo[1, at : at + OH]

    def source(t):
        taps = [xcol[n, t * B : (t + 1) * B].reshape(B * 2 * R, W) for n in (1, 2, 3)]
        line = lax.broadcasted_iota(jnp.int32, (2 * C - TAP_ROWS, W), 0)
        taps.append(jnp.where(jnp.logical_and(line >= 3 * t, line < 3 * t + 3), 1.0, 0.0))
        taps = jnp.concatenate(taps, axis=0).astype(BF16)
        src[t] = dot_nt(perm[...], taps).astype(BF16)

    edge_row = lax.broadcasted_iota(jnp.int32, (GRP, 2 * C), 0)

    def first(t, p):
        hidden = silu_of_half(dot(src[t], win_ref[p]))
        if p == 0:
            hidden = jnp.where(top, 0.0, hidden)
        if p == 5:
            hidden = jnp.where(bottom, 0.0, hidden)
        h1[t, p, GRP : GRP + W] = hidden.astype(BF16)
        before = pltpu.roll(hidden[W - GRP :], 1, 0)
        h1[t, p, :GRP] = jnp.where(edge_row > 0, before, 0.0).astype(BF16)
        after = pltpu.roll(hidden[:GRP], GRP - 1, 0)
        h1[t, p, GRP + W :] = jnp.where(edge_row < GRP - 1, after, 0.0).astype(BF16)

    lane = lax.broadcasted_iota(jnp.int32, (W, 2 * C), 1)

    def second(t, j):
        windows = jnp.concatenate(
            [h1[t, j + n, GRP * d : GRP * d + W] for d in range(3) for n in range(2)], axis=1
        )
        kept = jnp.concatenate(
            [h1[t, j, GRP : GRP + W, C:], h1[t, j + 1, GRP : GRP + W, :C]], axis=1
        ).astype(F32)
        hidden = kept + silu_of_half(dot(windows, wmid_ref[...]))
        if j == 0:
            hidden = jnp.where(jnp.logical_and(top, lane < C), 0.0, hidden)
        if j == 4:
            hidden = jnp.where(jnp.logical_and(bottom, lane >= C), 0.0, hidden)
        h2[t, :, 2 * C * j : 2 * C * (j + 1)] = hidden.astype(BF16)

    sub = lax.broadcasted_iota(jnp.int32, (R, LANES), 0)

    def blur(b):
        for at in range(0, W, LANES):
            cols = slice(at, at + LANES)
            for i in range(5):
                reach = sub < HALO + i - 2
                sums = [[0.0, 0.0] for _ in range(TH)]
                for j in range(5):
                    tap = 32 * b + 5 * i + j
                    up, own, down = (wts[n, tap : tap + 1, cols] for n in range(3))
                    w = (jnp.where(reach, up, own), jnp.where(reach, own, down))
                    for t in range(TH):
                        for n in range(2):
                            x = xcol[j, t * B + b, n * R : (n + 1) * R, cols]
                            sums[t][n] = sums[t][n] + w[n] * x
                for t in range(TH):
                    for n in range(2):
                        rows[t, i, n * R : (n + 1) * R, cols] = sums[t][n]
        inner = lax.broadcasted_iota(jnp.int32, (R + 2 * OH, W), 0)
        keep = jnp.logical_and(
            jnp.logical_or(inner >= OH, jnp.logical_not(top)),
            jnp.logical_or(inner < OH + R, jnp.logical_not(bottom)),
        )
        for t in range(TH):
            total = rows[t, 0, 0 : R + 2 * OH]
            for i in range(1, 5):
                total = total + rows[t, i, i : i + R + 2 * OH]
            mis[t * B + b] = jnp.where(keep, obs[b] - total, 0.0)

    guidance = {}

    def blur_back(b):
        for at in range(0, W, LANES):
            cols = slice(at, at + LANES)
            sums = [[0.0] * 5 for _ in range(TH)]
            for i in range(5):
                off = i - 2
                lines = [mis[t * B + b, OH - off : OH - off + R, cols] for t in range(TH)]
                for j in range(5):
                    tap = 32 * b + 5 * i + j
                    w = wts[1, tap : tap + 1, cols]
                    if off > 0:
                        w = jnp.where(sub < off, wts[0, tap : tap + 1, cols], w)
                    elif off < 0:
                        w = jnp.where(sub >= R + off, wts[2, tap : tap + 1, cols], w)
                    for t in range(TH):
                        sums[t][j] = sums[t][j] + w * lines[t]
            for t in range(TH):
                for j in range(5):
                    parts[t, j, :, cols] = sums[t][j]
        for t in range(TH):
            total = parts[t, 2]
            for j in (0, 1, 3, 4):
                total = total + shifted(parts[t, j], 2 - j)
            guidance[t, b] = total

    product = {}

    def third(t):
        both = dot(h2[t], wout_ref[...])
        high = both.astype(BF16)
        low = (both - high.astype(F32)).astype(BF16)
        product[t] = dot_tn(high, perm[...]) + dot_tn(low, perm[...])

    running = [None] * B

    def last(t):
        for b in range(B):
            score = 0.0
            for d in range(3):
                at = (d * B + b) * R
                score = score + shifted(product[t][at : at + R], d - 1)
            drift = (
                rate_ref[t : t + 1] * (score + guidance[t, b])
                + rate_ref[TH + t : TH + t + 1] * noise_ref[t, b]
            )
            running[b] = drift if t == 0 else running[b] + drift
            loc_ref[t, b] = start_ref[b] + running[b]
            if t == TH - 1:
                tot_ref[b] = running[b].astype(BF16)

    source(0)
    source(1)
    first(0, 0)
    first(0, 1)
    for t in range(TH):
        for j in range(5):
            second(t, j)
            if j < 4:
                first(t, j + 2)
            if j < B and t == 0:
                blur(j)
            if j == 1 and t == 1:
                third(0)
            if j < B and t == 1:
                blur_back(j)
        if t == 0:
            first(1, 0)
            first(1, 1)
    last(0)
    third(1)
    last(1)


def halo_routes(groups, count):
    def at(group, place):
        return group * count + place

    down, swap, up = [], [], []
    for g in range(groups):
        for i in range(count):
            other = at(g ^ 1, i)
            after = i + 1 if i < count - 1 else 2
            before = i - 1 if i > 2 else count - 1
            down.append((at(g, i), at(g, 1 - i if i < 2 else after)))
            swap.append((at(g, i), at(g, 3 - i) if i in (1, 2) else other))
            up.append((at(g, i), other if i < 2 else at(g, before)))
    return down, swap, up


def per_device(
    trajectory, noise, step_size, noise_scale, time_bias, start_state, observed,
    conv_in, conv_mid, conv_out, psf_bank, index_map,
):
    vmem = pl.BlockSpec(memory_space=pltpu.VMEM)
    smem = pl.BlockSpec(memory_space=pltpu.SMEM)
    hbm = pl.BlockSpec(memory_space=pltpu.HBM)
    packed = jax.ShapeDtypeStruct((PACK, W), BF16)
    send_f, send_s, send_b = pl.pallas_call(
        pack_kernel,
        out_shape=(packed, packed, packed),
        in_specs=[hbm, hbm],
        out_specs=(vmem, vmem, vmem),
        scratch_shapes=[
            pltpu.VMEM((TH, B, R, W), F32),
            pltpu.VMEM((B, R, W), F32),
            pltpu.VMEM((PACK, W), F32),
            pltpu.VMEM((PACK, W), F32),
            pltpu.SemaphoreType.DMA((2,)),
        ],
        cost_estimate=pl.CostEstimate(flops=2000000000, bytes_accessed=1000000, transcendentals=0),
        compiler_params=pltpu.CompilerParams(vmem_limit_bytes=60 * MIB),
    )(trajectory, observed)

    both = ("tm", "space")
    down, swap, up = halo_routes(lax.axis_size("tm"), lax.axis_size("space"))
    got_f = lax.ppermute(send_f, both, down)
    got_s = lax.ppermute(send_s, both, swap)
    got_b = lax.ppermute(send_b, both, up)

    tables = pl.pallas_call(
        tables_kernel,
        out_shape=(
            jax.ShapeDtypeStruct((W, W), BF16),
            jax.ShapeDtypeStruct((3, 32 * B, W), F32),
            jax.ShapeDtypeStruct((8, W), F32),
        ),
        in_specs=[vmem] * 3 + [smem] * 2,
        out_specs=(vmem,) * 3,
        scratch_shapes=[pltpu.VMEM((NPSF, 32 * B), F32)],
        cost_estimate=pl.CostEstimate(flops=2000000000, bytes_accessed=1000000, transcendentals=0),
        compiler_params=pltpu.CompilerParams(vmem_limit_bytes=8 * MIB),
    )(psf_bank, index_map, time_bias, step_size, noise_scale)
    weights = pl.pallas_call(
        weights_kernel,
        out_shape=(
            jax.ShapeDtypeStruct((6, 2 * C, 2 * C), BF16),
            jax.ShapeDtypeStruct((12 * C, 2 * C), BF16),
            jax.ShapeDtypeStruct((10 * C, C), BF16),
        ),
        in_specs=[vmem] * 4,
        out_specs=(vmem,) * 3,
        scratch_shapes=[
            pltpu.VMEM((6, 2 * C, 2 * C), F32),
            pltpu.VMEM((C, 10 * C), F32),
        ],
        cost_estimate=pl.CostEstimate(flops=2000000000, bytes_accessed=1000000, transcendentals=0),
        compiler_params=pltpu.CompilerParams(vmem_limit_bytes=8 * MIB),
    )(conv_in.transpose(0, 2, 1), conv_mid, conv_out, tables[2])

    local = jax.ShapeDtypeStruct((TH, B, R, W), F32)
    total = jax.ShapeDtypeStruct((B, R, W), BF16)
    loc, tot = pl.pallas_call(
        main_kernel,
        out_shape=(local, total),
        in_specs=[vmem] * 13,
        out_specs=(vmem, vmem),
        scratch_shapes=[
            pltpu.VMEM((5, TH * B, 2 * R, W), F32),
            pltpu.VMEM((B, R + 2 * OH, W), F32),
            pltpu.VMEM((TH, 5, 2 * R, W), F32),
            pltpu.VMEM((TH * B, R + 2 * OH, W), F32),
            pltpu.VMEM((TH, 5, R, W), F32),
            pltpu.VMEM((TH, W, 2 * C), BF16),
            pltpu.VMEM((TH, 6, W + 2 * GRP, 2 * C), BF16),
            pltpu.VMEM((TH, W, 10 * C), BF16),
            pltpu.VMEM((2, PACK, W), F32),
        ],
        cost_estimate=pl.CostEstimate(flops=8000000000, bytes_accessed=1000000, transcendentals=0),
        compiler_params=pltpu.CompilerParams(vmem_limit_bytes=24 * MIB),
    )(trajectory, noise, start_state, observed, got_f, got_s, got_b, *weights, *tables)

    m = lax.axis_size("tm")
    me = lax.axis_index("tm")
    before = 0.0
    for k in range(1, m):
        part = lax.ppermute(tot, "tm", [(i, (i + k) % m) for i in range(m)])
        before = before + jnp.where(me >= k, part.astype(F32), 0.0)
    return loc + before


def solution(mesh):
    return jax.shard_map(
        per_device,
        mesh=mesh,
        in_specs=(
            P("tm", None, "space", None),
            P("tm", None, "space", None),
            P("tm"),
            P("tm"),
            P("tm", None),
            P(None, "space", None),
            P(None, "space", None),
            P(),
            P(),
            P(),
            P(),
            P(),
        ),
        out_specs=P("tm", None, "space", None),
        check_vma=False,
    )
```

time: 37.6 us -> 28.1 us (0.75)
  the two profiles are of different devices: /device:TPU:6 before, /device:TPU:7 now
where the time goes in v2:
time: 28.1 us; the launch traced here: 28 us
  starting transfers between devices  11.9 us (42%)
  Pallas kernels  11.5 us (41%)
  waiting for transfers between devices  3.34 us (12%)
  other arithmetic  0.69 us (2%)
  local copies, waits for them, and re-layouts  0.45 us (2%)
    pallas_call x1, Pallas kernels, per_device(): pl.pallas_call(main_kernel, out_shape=(local, total), in_specs=[vmem] * 1...  8.2 us
    ppermute x1, starting transfers between devices, per_device(): got_b = lax.ppermute(send_b, both, up)  5.6 us
    ppermute x3, waiting for transfers between devices, per_device(): part = lax.ppermute(tot, 'tm', [(i, (i + k) % m) for i in range(m)])  3.34 us
    ppermute x1, starting transfers between devices, per_device(): got_f = lax.ppermute(send_f, both, down)  3.07 us
    ppermute x3, starting transfers between devices, per_device(): part = lax.ppermute(tot, 'tm', [(i, (i + k) % m) for i in range(m)])  2.24 us
    pallas_call x1, Pallas kernels, per_device(): pl.pallas_call(pack_kernel, out_shape=(packed, packed, packed), in_specs=...  1.62 us
    pallas_call x1, Pallas kernels, per_device(): pl.pallas_call(tables_kernel, out_shape=(jax.ShapeDtypeStruct((W, W), BF1...  1.17 us
    ppermute x1, starting transfers between devices, per_device(): got_s = lax.ppermute(send_s, both, swap)  0.96 us
  transfers between devices with their start and end apart: 6, of which 3 were waited for; matrix products, arithmetic and copies ran while one was open for 0% of the time, Pallas kernels for 6%

profile of v2, /device:TPU:7, one launch (start us, length us, event | category | flops | bytes accessed | tf_op | source)
XLA Modules:
  0.0 28.0 jit_solution(14322056842143118231)
XLA Ops:
  0.0 1.6 %shard_map.118 = (bf16[40,512]{1,0:T(8,128)(2,1)}, bf16[40,512]{1,0:T(8,128)(2,1)}, bf16[40,512]{1,0:T(8,128)(2,1)}) custom-call(f32[2,4,8,512]{3,2,1,0:T(8,128)} %x_ref.1, f32[4,8,512]{2,1,0:T(8,128)} %obs_ref.1), custom_call_target="tpu_custom_call" | custom-call | flops 2000000000 | bytes 1000000 | tf_op jit(solution)/shard_map/pallas_call | solution.py:358
  1.6 3.1 %collective-permute-start = (bf16[40,512]{1,0:T(8,128)(2,1)}, bf16[40,512]{1,0:T(8,128)(2,1)S(1)}, u32[]{:S(2)}, u32[]{:S(2)}) collective-permute-start(bf16[40,512]{1,0:T(8,128)(2,1)} %get-tuple-element.16), channel_id=1, source_target_pairs={{0,1},{1,0},{2,3},{3,4},{4,5},{5,6},{6,7},{7,8},{8,9},{9,10},{10,1... | collective-permute-start | bytes 122888 | tf_op jit(solution)/shard_map/ppermute | solution.py:376
  4.7 1.0 %collective-permute-start.1 = (bf16[40,512]{1,0:T(8,128)(2,1)}, bf16[40,512]{1,0:T(8,128)(2,1)S(1)}, u32[]{:S(2)}, u32[]{:S(2)}) collective-permute-start(bf16[40,512]{1,0:T(8,128)(2,1)} %get-tuple-element.17), channel_id=1, source_target_pairs={{0,64},{1,2},{2,1},{3,67},{4,68},{5,69},{6,70},{7,71},{8,72},{9,73... | collective-permute-start | bytes 122888 | tf_op jit(solution)/shard_map/ppermute | solution.py:377
  5.7 5.6 %collective-permute-start.2 = (bf16[40,512]{1,0:T(8,128)(2,1)}, bf16[40,512]{1,0:T(8,128)(2,1)S(1)}, u32[]{:S(2)}, u32[]{:S(2)}) collective-permute-start(bf16[40,512]{1,0:T(8,128)(2,1)} %get-tuple-element.18), channel_id=1, source_target_pairs={{0,64},{1,65},{2,63},{3,2},{4,3},{5,4},{6,5},{7,6},{8,7},{9,8},{10... | collective-permute-start | bytes 122888 | tf_op jit(solution)/shard_map/ppermute | solution.py:378
  11.3 0.0 copy-done.5
  11.3 0.0 copy-done.6
  11.3 0.0 copy-done.11
  11.3 0.0 copy-done.9
  11.3 0.0 copy-done.10
  11.3 1.2 %shard_map.119 = (bf16[512,512]{1,0:T(8,128)(2,1)S(1)}, f32[3,128,512]{2,1,0:T(8,128)S(1)}, f32[8,512]{1,0:T(8,128)S(1)}) custom-call(f32[16,4,25]{2,1,0:T(4,128)S(1)} %copy-done.5, s32[64,64]{1,0:T(8,128)S(1)} %copy-done.6, f32[2,128]{1,0:T(2,128)S(1)} %copy-done.9, f32[2]{0:T(128)S(1)} %copy-done.10, f32[2]{0:T(128)S(1)} %copy-done.11), custom_call_target="tpu_custom_call" | custom-call | flops 2000000000 | bytes 1000000 | tf_op jit(solution)/shard_map/pallas_call | solution.py:380
  12.5 0.0 copy-done
  12.5 0.0 copy-done.7
  12.5 0.0 copy-done.8
  12.5 0.0 copy-start.1
  12.5 0.0 copy-start.2
  12.5 0.0 copy-start.3
  12.5 0.0 copy-start.4
  12.5 0.5 %shard_map.120 = (bf16[6,256,256]{2,1,0:T(8,128)(2,1)S(1)}, bf16[1536,256]{1,0:T(8,128)(2,1)S(1)}, bf16[1280,128]{1,0:T(8,128)(2,1)S(1)}) custom-call(bf16[9,4,128]{2,1,0:T(4,128)(2,1)S(1)} %bitcast.1, bf16[9,128,128]{2,1,0:T(8,128)(2,1)S(1)} %copy-done, bf16[9,4,128]{2,1,0:T(4,128)(2,1)S(1)} %copy-done.8, f32[8,512]{1,0:T(8,128)S(1)} %get-tuple-element.19.rate_ref), custom_call_target="tpu_custom_call" | custom-call | flops 2000000000 | bytes 1000000 | tf_op jit(solution)/shard_map/pallas_call | solution.py:393
  13.1 0.0 collective-permute-done.f_ref
  13.1 0.0 collective-permute-done.1.s_ref
  13.1 0.0 collective-permute-done.2.b_ref
  13.1 0.3 %copy-done.1 = f32[2,4,8,512]{3,2,1,0:T(8,128)S(1)} copy-done((f32[2,4,8,512]{3,2,1,0:T(8,128)S(1)}, f32[2,4,8,512]{3,2,1,0:T(8,128)}, u32[]{:S(2)}) %copy-start.1) | copy-done | bytes 131096
  13.4 0.1 copy-done.2
  13.5 0.0 copy-done.4
  13.5 8.2 %shard_map.121 = (f32[2,4,8,512]{3,2,1,0:T(8,128)S(1)}, bf16[4,8,512]{2,1,0:T(8,128)(2,1)S(1)}) custom-call(f32[2,4,8,512]{3,2,1,0:T(8,128)S(1)} %copy-done.1, f32[2,4,8,512]{3,2,1,0:T(8,128)S(1)} %copy-done.2, f32[4,8,512]{2,1,0:T(8,128)S(1)} %copy-done.3, f32[4,8,512]{2,1,0:T(8,128)S(1)} %copy-done.4, bf16[40,512]{1,0:T(8,128)(2,1)S(1)} %collective-permute-done.f_ref, ...), custom_call_target="tpu_custom_call" | custom-call | flops 8000000000 | bytes 1000000 | tf_op jit(solution)/shard_map/pallas_call | solution.py:412
  21.7 1.3 %collective-permute-start.3 = (bf16[4,8,512]{2,1,0:T(8,128)(2,1)S(1)}, bf16[4,8,512]{2,1,0:T(8,128)(2,1)S(1)}, u32[]{:S(2)}, u32[]{:S(2)}) collective-permute-start(bf16[4,8,512]{2,1,0:T(8,128)(2,1)S(1)} %get-tuple-element.26), channel_id=1, source_target_pairs={{0,64},{64,128},{128,192},{192,0},{1,65},{65,129},{129,193},{193,1... | collective-permute-start | bytes 98312 | tf_op jit(solution)/shard_map/ppermute | solution.py:436
  23.0 0.9 %collective-permute-start.4 = (bf16[4,8,512]{2,1,0:T(8,128)(2,1)S(1)}, bf16[4,8,512]{2,1,0:T(8,128)(2,1)S(1)}, u32[]{:S(2)}, u32[]{:S(2)}) collective-permute-start(bf16[4,8,512]{2,1,0:T(8,128)(2,1)S(1)} %get-tuple-element.26), channel_id=1, source_target_pairs={{0,128},{64,192},{128,0},{192,64},{1,129},{65,193},{129,1},{193,65... | collective-permute-start | bytes 98312 | tf_op jit(solution)/shard_map/ppermute | solution.py:436
  23.9 0.0 collective-permute-start.5
  23.9 0.1 collective-permute-done.3
  24.0 2.3 %collective-permute-done.4 = bf16[4,8,512]{2,1,0:T(8,128)(2,1)S(1)} collective-permute-done((bf16[4,8,512]{2,1,0:T(8,128)(2,1)S(1)}, bf16[4,8,512]{2,1,0:T(8,128)(2,1)S(1)}, u32[]{:S(2)}, u32[]{:S(2)}) %collective-permute-start.4) | collective-permute-done | bytes 32800 | tf_op jit(solution)/shard_map/ppermute | solution.py:436
  26.3 1.0 %collective-permute-done.5 = bf16[4,8,512]{2,1,0:T(8,128)(2,1)S(1)} collective-permute-done((bf16[4,8,512]{2,1,0:T(8,128)(2,1)S(1)}, bf16[4,8,512]{2,1,0:T(8,128)(2,1)S(1)}, u32[]{:S(2)}, u32[]{:S(2)}) %collective-permute-start.5) | collective-permute-done | bytes 32800 | tf_op jit(solution)/shard_map/ppermute | solution.py:436
  27.3 0.7 %broadcast_add_fusion = f32[2,4,8,512]{3,2,1,0:T(8,128)} fusion(f32[2,4,8,512]{3,2,1,0:T(8,128)S(1)} %get-tuple-element.25, f32[4,8,512]{2,1,0:T(8,128)S(1)} %select_add_fusion), kind=kLoop, calls=%fused_computation | loop fusion | flops 32768 | bytes 327680 | tf_op jit(solution)/shard_map/add | solution.py:438
  (10 shorter events, 0.0 us)
Async XLA Ops:
  0.0 11.3 %copy-start.5 = (f32[16,4,25]{2,1,0:T(4,128)S(1)}, f32[16,4,25]{2,1,0:T(4,128)}, u32[]{:S(2)}) copy-start(f32[16,4,25]{2,1,0:T(4,128)} %psf_ref.1) | copy-start | bytes 19204
  0.0 11.3 %copy-start.6 = (s32[64,64]{1,0:T(8,128)S(1)}, s32[64,64]{1,0:T(8,128)}, u32[]{:S(2)}) copy-start(s32[64,64]{1,0:T(8,128)} %map_ref.1) | copy-start | bytes 49156
  1.6 11.4 %collective-permute-start = (bf16[40,512]{1,0:T(8,128)(2,1)}, bf16[40,512]{1,0:T(8,128)(2,1)S(1)}, u32[]{:S(2)}, u32[]{:S(2)}) collective-permute-start(bf16[40,512]{1,0:T(8,128)(2,1)} %get-tuple-element.16), channel_id=1, source_target_pairs={{0,1},{1,0},{2,3},{3,4},{4,5},{5,6},{6,7},{7,8},{8,9},{9,10},{10,1... | collective-permute-start | bytes 122888 | tf_op jit(solution)/shard_map/ppermute | solution.py:376
  4.7 6.6 %copy-start.11 = (f32[2]{0:T(128)S(1)}, f32[2]{0:T(128)}, u32[]{:S(2)}) copy-start(f32[2]{0:T(128)} %scale_ref.1) | copy-start | bytes 28
  4.7 6.6 %copy-start.9 = (f32[2,128]{1,0:T(2,128)S(1)}, f32[2,128]{1,0:T(2,128)}, u32[]{:S(2)}) copy-start(f32[2,128]{1,0:T(2,128)} %bias_ref.1) | copy-start | bytes 3076
  4.7 6.6 %copy-start.10 = (f32[2]{0:T(128)S(1)}, f32[2]{0:T(128)}, u32[]{:S(2)}) copy-start(f32[2]{0:T(128)} %step_ref.1) | copy-start | bytes 28
  4.7 8.4 %collective-permute-start.1 = (bf16[40,512]{1,0:T(8,128)(2,1)}, bf16[40,512]{1,0:T(8,128)(2,1)S(1)}, u32[]{:S(2)}, u32[]{:S(2)}) collective-permute-start(bf16[40,512]{1,0:T(8,128)(2,1)} %get-tuple-element.17), channel_id=1, source_target_pairs={{0,64},{1,2},{2,1},{3,67},{4,68},{5,69},{6,70},{7,71},{8,72},{9,73... | collective-permute-start | bytes 122888 | tf_op jit(solution)/shard_map/ppermute | solution.py:377
  5.7 6.8 %copy-start = (bf16[9,128,128]{2,1,0:T(8,128)(2,1)S(1)}, bf16[9,128,128]{2,1,0:T(8,128)(2,1)}, u32[]{:S(2)}) copy-start(bf16[9,128,128]{2,1,0:T(8,128)(2,1)} %wmid_raw.1) | copy-start | bytes 884740
  5.7 6.8 %copy-start.7 = (bf16[9,128,4]{1,2,0:T(4,128)(2,1)S(1)}, bf16[9,128,4]{1,2,0:T(4,128)(2,1)}, u32[]{:S(2)}) copy-start(bf16[9,128,4]{1,2,0:T(4,128)(2,1)} %param.19) | copy-start | bytes 27652
  5.7 6.8 %copy-start.8 = (bf16[9,4,128]{2,1,0:T(4,128)(2,1)S(1)}, bf16[9,4,128]{2,1,0:T(4,128)(2,1)}, u32[]{:S(2)}) copy-start(bf16[9,4,128]{2,1,0:T(4,128)(2,1)} %wout_raw.1) | copy-start | bytes 27652
  5.7 7.4 %collective-permute-start.2 = (bf16[40,512]{1,0:T(8,128)(2,1)}, bf16[40,512]{1,0:T(8,128)(2,1)S(1)}, u32[]{:S(2)}, u32[]{:S(2)}) collective-permute-start(bf16[40,512]{1,0:T(8,128)(2,1)} %get-tuple-element.18), channel_id=1, source_target_pairs={{0,64},{1,65},{2,63},{3,2},{4,3},{5,4},{6,5},{7,6},{8,7},{9,8},{10... | collective-permute-start | bytes 122888 | tf_op jit(solution)/shard_map/ppermute | solution.py:378
  12.5 0.9 %copy-start.1 = (f32[2,4,8,512]{3,2,1,0:T(8,128)S(1)}, f32[2,4,8,512]{3,2,1,0:T(8,128)}, u32[]{:S(2)}) copy-start(f32[2,4,8,512]{3,2,1,0:T(8,128)} %x_ref.1) | copy-start | bytes 393220
  12.5 1.0 %copy-start.2 = (f32[2,4,8,512]{3,2,1,0:T(8,128)S(1)}, f32[2,4,8,512]{3,2,1,0:T(8,128)}, u32[]{:S(2)}) copy-start(f32[2,4,8,512]{3,2,1,0:T(8,128)} %noise_ref.1) | copy-start | bytes 393220
  12.5 1.0 %copy-start.3 = (f32[4,8,512]{2,1,0:T(8,128)S(1)}, f32[4,8,512]{2,1,0:T(8,128)}, u32[]{:S(2)}) copy-start(f32[4,8,512]{2,1,0:T(8,128)} %start_ref.1) | copy-start | bytes 196612
  12.5 1.0 %copy-start.4 = (f32[4,8,512]{2,1,0:T(8,128)S(1)}, f32[4,8,512]{2,1,0:T(8,128)}, u32[]{:S(2)}) copy-start(f32[4,8,512]{2,1,0:T(8,128)} %obs_ref.1) | copy-start | bytes 196612
  21.7 2.3 %collective-permute-start.3 = (bf16[4,8,512]{2,1,0:T(8,128)(2,1)S(1)}, bf16[4,8,512]{2,1,0:T(8,128)(2,1)S(1)}, u32[]{:S(2)}, u32[]{:S(2)}) collective-permute-start(bf16[4,8,512]{2,1,0:T(8,128)(2,1)S(1)} %get-tuple-element.26), channel_id=1, source_target_pairs={{0,64},{64,128},{128,192},{192,0},{1,65},{65,129},{129,193},{193,1... | collective-permute-start | bytes 98312 | tf_op jit(solution)/shard_map/ppermute | solution.py:436
  23.0 3.3 %collective-permute-start.4 = (bf16[4,8,512]{2,1,0:T(8,128)(2,1)S(1)}, bf16[4,8,512]{2,1,0:T(8,128)(2,1)S(1)}, u32[]{:S(2)}, u32[]{:S(2)}) collective-permute-start(bf16[4,8,512]{2,1,0:T(8,128)(2,1)S(1)} %get-tuple-element.26), channel_id=1, source_target_pairs={{0,128},{64,192},{128,0},{192,64},{1,129},{65,193},{129,1},{193,65... | collective-permute-start | bytes 98312 | tf_op jit(solution)/shard_map/ppermute | solution.py:436
  23.9 3.3 %collective-permute-start.5 = (bf16[4,8,512]{2,1,0:T(8,128)(2,1)S(1)}, bf16[4,8,512]{2,1,0:T(8,128)(2,1)S(1)}, u32[]{:S(2)}, u32[]{:S(2)}) collective-permute-start(bf16[4,8,512]{2,1,0:T(8,128)(2,1)S(1)} %get-tuple-element.26), channel_id=1, source_target_pairs={{0,192},{64,0},{128,64},{192,128},{1,193},{65,1},{129,65},{193,129... | collective-permute-start | bytes 98312 | tf_op jit(solution)/shard_map/ppermute | solution.py:436

commit v3 on v2

--- a/solution.py
+++ b/solution.py
@@ -14,7 +14,6 @@
 TH = 2
 HALO = 4
 OH = 2
-PACK = TH * B * HALO + B * OH
 LANES = 128
 GRP = 16
 STR = W // GRP
@@ -47,32 +46,6 @@
     moved = pltpu.roll(v, (-by) % W, v.ndim - 1)
     inside = lane < W - by if by > 0 else lane >= -by
     return jnp.where(inside, moved, 0.0)
-
-
-def pack_kernel(x_hbm, obs_hbm, f_ref, s_ref, b_ref, x, obs, head, tail, sems):
-    copies = [
-        pltpu.make_async_copy(x_hbm, x, sems.at[0]),
-        pltpu.make_async_copy(obs_hbm, obs, sems.at[1]),
-    ]
-    for copy in copies:
-        copy.start()
-    second = lax.axis_index("space") == 1
-    for copy in copies:
-        copy.wait()
-    for t in range(TH):
-        for b in range(B):
-            at = (t * B + b) * HALO
-            head[at : at + HALO] = x[t, b, :HALO]
-            tail[at : at + HALO] = x[t, b, R - HALO :]
-    for b in range(B):
-        at = TH * B * HALO + b * OH
-        head[at : at + OH] = obs[b, :OH]
-        tail[at : at + OH] = obs[b, R - OH :]
-    first, last = head[...], tail[...]
-    f_ref[...] = jnp.where(second, first, last).astype(BF16)
-    rest = jnp.where(second, last, first).astype(BF16)
-    s_ref[...] = rest
-    b_ref[...] = rest
 
 
 def tables_kernel(
@@ -178,16 +151,15 @@
     below = jnp.where(top, got_f, jnp.where(place == 1, got_s, got_b))
     halo[1] = jnp.where(bottom, 0.0, below)
     for k in range(TH * B):
-        xcol[2, k, 0:HALO] = halo[0, k * HALO : (k + 1) * HALO]
+        xcol[2, k, 0:HALO] = halo[0, k]
         xcol[2, k, HALO : HALO + R] = x_ref[k // B, k % B]
-        xcol[2, k, HALO + R :] = halo[1, k * HALO : (k + 1) * HALO]
-        for n in (0, 1, 3, 4):
+        xcol[2, k, HALO + R :] = halo[1, k]
+        for n in (1, 3):
             xcol[n, k] = shifted(xcol[2, k], n - 2)
     for b in range(B):
-        at = TH * B * HALO + b * OH
-        obs[b, 0:OH] = halo[0, at : at + OH]
+        obs[b, 0:OH] = halo[0, TH * B + b, HALO - OH :]
         obs[b, OH : OH + R] = obs_ref[b]
-        obs[b, OH + R : 2 * OH + R] = halo[1, at : at + OH]
+        obs[b, OH + R : 2 * OH + R] = halo[1, TH * B + b, :OH]
 
     def source(t):
         taps = [xcol[n, t * B : (t + 1) * B].reshape(B * 2 * R, W) for n in (1, 2, 3)]
@@ -312,6 +284,9 @@
     source(1)
     first(0, 0)
     first(0, 1)
+    for k in range(TH * B):
+        for n in (0, 4):
+            xcol[n, k] = shifted(xcol[2, k], n - 2)
     for t in range(TH):
         for j in range(5):
             second(t, j)
@@ -353,23 +328,12 @@
 ):
     vmem = pl.BlockSpec(memory_space=pltpu.VMEM)
     smem = pl.BlockSpec(memory_space=pltpu.SMEM)
-    hbm = pl.BlockSpec(memory_space=pltpu.HBM)
-    packed = jax.ShapeDtypeStruct((PACK, W), BF16)
-    send_f, send_s, send_b = pl.pallas_call(
-        pack_kernel,
-        out_shape=(packed, packed, packed),
-        in_specs=[hbm, hbm],
-        out_specs=(vmem, vmem, vmem),
-        scratch_shapes=[
-            pltpu.VMEM((TH, B, R, W), F32),
-            pltpu.VMEM((B, R, W), F32),
-            pltpu.VMEM((PACK, W), F32),
-            pltpu.VMEM((PACK, W), F32),
-            pltpu.SemaphoreType.DMA((2,)),
-        ],
-        cost_estimate=pl.CostEstimate(flops=2000000000, bytes_accessed=1000000, transcendentals=0),
-        compiler_params=pltpu.CompilerParams(vmem_limit_bytes=60 * MIB),
-    )(trajectory, observed)
+    second = lax.axis_index("space") == 1
+    cells = jnp.concatenate([trajectory.reshape(TH * B, R, W), observed])
+    head, tail = cells[:, :HALO], cells[:, R - HALO :]
+    send_f = jnp.where(second, head, tail).astype(BF16)
+    send_s = jnp.where(second, tail, head).astype(BF16)
+    send_b = head.astype(BF16)
 
     both = ("tm", "space")
     down, swap, up = halo_routes(lax.axis_size("tm"), lax.axis_size("space"))
@@ -423,7 +387,7 @@
             pltpu.VMEM((TH, W, 2 * C), BF16),
             pltpu.VMEM((TH, 6, W + 2 * GRP, 2 * C), BF16),
             pltpu.VMEM((TH, W, 10 * C), BF16),
-            pltpu.VMEM((2, PACK, W), F32),
+            pltpu.VMEM((2, TH * B + B, HALO, W), F32),
         ],
         cost_estimate=pl.CostEstimate(flops=8000000000, bytes_accessed=1000000, transcendentals=0),
         compiler_params=pltpu.CompilerParams(vmem_limit_bytes=24 * MIB),

time: 28.1 us -> 27.8 us (0.989)
  Pallas kernels: 11.5 us -> 9.85 us
  other arithmetic: 0.69 us -> 2 us
    pallas_call x1 -> x0, Pallas kernels: 1.62 us -> none  [per_device(): pl.pallas_call(pack_kernel, out_shape=(packed, packed, packed), in_specs=...]
    convert_element_type x0 -> x1, other arithmetic: none -> 1.31 us  [per_device(): send_b = head.astype(BF16)]
where the time goes in v3:
time: 27.8 us; the launch traced here: 27.7 us
  starting transfers between devices  11.9 us (43%)
  Pallas kernels  9.85 us (35%)
  waiting for transfers between devices  3.34 us (12%)
  other arithmetic  2 us (7%)
  local copies, waits for them, and re-layouts  0.46 us (2%)
    pallas_call x1, Pallas kernels, per_device(): pl.pallas_call(main_kernel, out_shape=(local, total), in_specs=[vmem] * 1...  8.18 us
    ppermute x1, starting transfers between devices, per_device(): got_b = lax.ppermute(send_b, both, up)  5.6 us
    ppermute x3, waiting for transfers between devices, per_device(): part = lax.ppermute(tot, 'tm', [(i, (i + k) % m) for i in range(m)])  3.34 us
    ppermute x1, starting transfers between devices, per_device(): got_f = lax.ppermute(send_f, both, down)  3.07 us
    ppermute x3, starting transfers between devices, per_device(): part = lax.ppermute(tot, 'tm', [(i, (i + k) % m) for i in range(m)])  2.26 us
    convert_element_type x1, other arithmetic, per_device(): send_b = head.astype(BF16)  1.31 us
    pallas_call x1, Pallas kernels, per_device(): pl.pallas_call(tables_kernel, out_shape=(jax.ShapeDtypeStruct((W, W), BF1...  1.17 us
    ppermute x1, starting transfers between devices, per_device(): got_s = lax.ppermute(send_s, both, swap)  0.96 us
  transfers between devices with their start and end apart: 6, of which 3 were waited for; matrix products, arithmetic and copies ran while one was open for 0% of the time, Pallas kernels for 6%

profile of v3, /device:TPU:7, one launch (start us, length us, event | category | flops | bytes accessed | tf_op | source)
XLA Modules:
  0.0 27.7 jit_solution(13577304186747965262)
XLA Ops:
  0.0 1.3 %fusion.1 = (bf16[12,4,512]{2,1,0:T(4,128)(2,1)S(1)}, bf16[12,4,512]{2,1,0:T(4,128)(2,1)S(1)}, bf16[12,4,512]{2,1,0:T(4,128)(2,1)S(1)}) fusion(f32[4,8,512]{2,1,0:T(8,128)} %obs_ref.1, f32[8,8,512]{2,1,0:T(8,128)} %bitcast.2, pred[]{:T(512)S(6)} %eq.3), kind=kLoop, calls=%fused_computation.8 | loop fusion | flops 442368 | bytes 344065 | tf_op jit(solution)/shard_map/convert_element_type | solution.py:336
  1.3 3.1 %collective-permute-start = (bf16[12,4,512]{2,1,0:T(4,128)(2,1)S(1)}, bf16[12,4,512]{2,1,0:T(4,128)(2,1)S(1)}, u32[]{:S(2)}, u32[]{:S(2)}) collective-permute-start(bf16[12,4,512]{2,1,0:T(4,128)(2,1)S(1)} %get-tuple-element.22), channel_id=1, source_target_pairs={{0,1},{1,0},{2,3},{3,4},{4,5},{5,6},{6,7},{7,8},{8,9},{9,10},{10,1... | collective-permute-start | bytes 147464 | tf_op jit(solution)/shard_map/ppermute | solution.py:340
  4.4 1.0 %collective-permute-start.1 = (bf16[12,4,512]{2,1,0:T(4,128)(2,1)S(1)}, bf16[12,4,512]{2,1,0:T(4,128)(2,1)S(1)}, u32[]{:S(2)}, u32[]{:S(2)}) collective-permute-start(bf16[12,4,512]{2,1,0:T(4,128)(2,1)S(1)} %get-tuple-element.23), channel_id=1, source_target_pairs={{0,64},{1,2},{2,1},{3,67},{4,68},{5,69},{6,70},{7,71},{8,72},{9,73... | collective-permute-start | bytes 147464 | tf_op jit(solution)/shard_map/ppermute | solution.py:341
  5.4 5.6 %collective-permute-start.2 = (bf16[12,4,512]{2,1,0:T(4,128)(2,1)S(1)}, bf16[12,4,512]{2,1,0:T(4,128)(2,1)S(1)}, u32[]{:S(2)}, u32[]{:S(2)}) collective-permute-start(bf16[12,4,512]{2,1,0:T(4,128)(2,1)S(1)} %get-tuple-element.21), channel_id=1, source_target_pairs={{0,64},{1,65},{2,63},{3,2},{4,3},{5,4},{6,5},{7,6},{8,7},{9,8},{10... | collective-permute-start | bytes 147464 | tf_op jit(solution)/shard_map/ppermute | solution.py:342
  11.0 0.0 copy-done.5
  11.0 0.0 copy-done.6
  11.0 0.0 copy-done.11
  11.0 0.0 copy-done.9
  11.0 0.0 copy-done.10
  11.0 1.2 %shard_map.118 = (bf16[512,512]{1,0:T(8,128)(2,1)S(1)}, f32[3,128,512]{2,1,0:T(8,128)S(1)}, f32[8,512]{1,0:T(8,128)S(1)}) custom-call(f32[16,4,25]{2,1,0:T(4,128)S(1)} %copy-done.5, s32[64,64]{1,0:T(8,128)S(1)} %copy-done.6, f32[2,128]{1,0:T(2,128)S(1)} %copy-done.9, f32[2]{0:T(128)S(1)} %copy-done.10, f32[2]{0:T(128)S(1)} %copy-done.11), custom_call_target="tpu_custom_call" | custom-call | flops 2000000000 | bytes 1000000 | tf_op jit(solution)/shard_map/pallas_call | solution.py:344
  12.1 0.0 copy-done.2
  12.2 0.0 copy-done.7
  12.2 0.0 copy-done.8
  12.2 0.0 copy-start
  12.2 0.0 copy-start.1
  12.2 0.0 copy-start.3
  12.2 0.0 copy-start.4
  12.2 0.5 %shard_map.119 = (bf16[6,256,256]{2,1,0:T(8,128)(2,1)S(1)}, bf16[1536,256]{1,0:T(8,128)(2,1)S(1)}, bf16[1280,128]{1,0:T(8,128)(2,1)S(1)}) custom-call(bf16[9,4,128]{2,1,0:T(4,128)(2,1)S(1)} %bitcast.3, bf16[9,128,128]{2,1,0:T(8,128)(2,1)S(1)} %copy-done.2, bf16[9,4,128]{2,1,0:T(4,128)(2,1)S(1)} %copy-done.8, f32[8,512]{1,0:T(8,128)S(1)} %get-tuple-element.13.rate_ref), custom_call_target="tpu_custom_call" | custom-call | flops 2000000000 | bytes 1000000 | tf_op jit(solution)/shard_map/pallas_call | solution.py:357
  12.7 0.0 collective-permute-done.f_ref
  12.7 0.0 collective-permute-done.1.s_ref
  12.8 0.0 collective-permute-done.2.b_ref
  12.8 0.3 %copy-done = f32[2,4,8,512]{3,2,1,0:T(8,128)S(1)} copy-done((f32[2,4,8,512]{3,2,1,0:T(8,128)S(1)}, f32[2,4,8,512]{3,2,1,0:T(8,128)}, u32[]{:S(2)}) %copy-start) | copy-done | bytes 131096
  13.1 0.1 copy-done.3
  13.2 0.0 copy-done.4
  13.2 8.2 %shard_map.120 = (f32[2,4,8,512]{3,2,1,0:T(8,128)S(1)}, bf16[4,8,512]{2,1,0:T(8,128)(2,1)S(1)}) custom-call(f32[2,4,8,512]{3,2,1,0:T(8,128)S(1)} %copy-done, f32[2,4,8,512]{3,2,1,0:T(8,128)S(1)} %copy-done.3, f32[4,8,512]{2,1,0:T(8,128)S(1)} %copy-done.4, f32[4,8,512]{2,1,0:T(8,128)S(1)} %copy-done.1, bf16[12,4,512]{2,1,0:T(4,128)(2,1)S(1)} %collective-permute-done.f_ref, ...), custom_call_target="tpu_custom_call" | custom-call | flops 8000000000 | bytes 1000000 | tf_op jit(solution)/shard_map/pallas_call | solution.py:376
  21.4 1.4 %collective-permute-start.3 = (bf16[4,8,512]{2,1,0:T(8,128)(2,1)S(1)}, bf16[4,8,512]{2,1,0:T(8,128)(2,1)S(1)}, u32[]{:S(2)}, u32[]{:S(2)}) collective-permute-start(bf16[4,8,512]{2,1,0:T(8,128)(2,1)S(1)} %get-tuple-element.20), channel_id=1, source_target_pairs={{0,64},{64,128},{128,192},{192,0},{1,65},{65,129},{129,193},{193,1... | collective-permute-start | bytes 98312 | tf_op jit(solution)/shard_map/ppermute | solution.py:400
  22.8 0.8 %collective-permute-start.4 = (bf16[4,8,512]{2,1,0:T(8,128)(2,1)S(1)}, bf16[4,8,512]{2,1,0:T(8,128)(2,1)S(1)}, u32[]{:S(2)}, u32[]{:S(2)}) collective-permute-start(bf16[4,8,512]{2,1,0:T(8,128)(2,1)S(1)} %get-tuple-element.20), channel_id=1, source_target_pairs={{0,128},{64,192},{128,0},{192,64},{1,129},{65,193},{129,1},{193,65... | collective-permute-start | bytes 98312 | tf_op jit(solution)/shard_map/ppermute | solution.py:400
  23.6 0.0 collective-permute-start.5
  23.6 0.2 collective-permute-done.3
  23.8 2.4 %collective-permute-done.4 = bf16[4,8,512]{2,1,0:T(8,128)(2,1)S(1)} collective-permute-done((bf16[4,8,512]{2,1,0:T(8,128)(2,1)S(1)}, bf16[4,8,512]{2,1,0:T(8,128)(2,1)S(1)}, u32[]{:S(2)}, u32[]{:S(2)}) %collective-permute-start.4) | collective-permute-done | bytes 32800 | tf_op jit(solution)/shard_map/ppermute | solution.py:400
  26.2 0.8 %collective-permute-done.5 = bf16[4,8,512]{2,1,0:T(8,128)(2,1)S(1)} collective-permute-done((bf16[4,8,512]{2,1,0:T(8,128)(2,1)S(1)}, bf16[4,8,512]{2,1,0:T(8,128)(2,1)S(1)}, u32[]{:S(2)}, u32[]{:S(2)}) %collective-permute-start.5) | collective-permute-done | bytes 32800 | tf_op jit(solution)/shard_map/ppermute | solution.py:400
  27.0 0.7 %broadcast_add_fusion = f32[2,4,8,512]{3,2,1,0:T(8,128)} fusion(f32[2,4,8,512]{3,2,1,0:T(8,128)S(1)} %get-tuple-element.19, f32[4,8,512]{2,1,0:T(8,128)S(1)} %select_add_fusion), kind=kLoop, calls=%fused_computation.6 | loop fusion | flops 32768 | bytes 327680 | tf_op jit(solution)/shard_map/add | solution.py:402
  (10 shorter events, 0.0 us)
Async XLA Ops:
  0.0 11.0 %copy-start.5 = (f32[16,4,25]{2,1,0:T(4,128)S(1)}, f32[16,4,25]{2,1,0:T(4,128)}, u32[]{:S(2)}) copy-start(f32[16,4,25]{2,1,0:T(4,128)} %psf_ref.1) | copy-start | bytes 19204
  0.0 11.0 %copy-start.6 = (s32[64,64]{1,0:T(8,128)S(1)}, s32[64,64]{1,0:T(8,128)}, u32[]{:S(2)}) copy-start(s32[64,64]{1,0:T(8,128)} %map_ref.1) | copy-start | bytes 49156
  1.3 11.4 %collective-permute-start = (bf16[12,4,512]{2,1,0:T(4,128)(2,1)S(1)}, bf16[12,4,512]{2,1,0:T(4,128)(2,1)S(1)}, u32[]{:S(2)}, u32[]{:S(2)}) collective-permute-start(bf16[12,4,512]{2,1,0:T(4,128)(2,1)S(1)} %get-tuple-element.22), channel_id=1, source_target_pairs={{0,1},{1,0},{2,3},{3,4},{4,5},{5,6},{6,7},{7,8},{8,9},{9,10},{10,1... | collective-permute-start | bytes 147464 | tf_op jit(solution)/shard_map/ppermute | solution.py:340
  4.4 6.6 %copy-start.11 = (f32[2]{0:T(128)S(1)}, f32[2]{0:T(128)}, u32[]{:S(2)}) copy-start(f32[2]{0:T(128)} %scale_ref.1) | copy-start | bytes 28
  4.4 6.6 %copy-start.9 = (f32[2,128]{1,0:T(2,128)S(1)}, f32[2,128]{1,0:T(2,128)}, u32[]{:S(2)}) copy-start(f32[2,128]{1,0:T(2,128)} %bias_ref.1) | copy-start | bytes 3076
  4.4 6.6 %copy-start.10 = (f32[2]{0:T(128)S(1)}, f32[2]{0:T(128)}, u32[]{:S(2)}) copy-start(f32[2]{0:T(128)} %step_ref.1) | copy-start | bytes 28
  4.4 8.4 %collective-permute-start.1 = (bf16[12,4,512]{2,1,0:T(4,128)(2,1)S(1)}, bf16[12,4,512]{2,1,0:T(4,128)(2,1)S(1)}, u32[]{:S(2)}, u32[]{:S(2)}) collective-permute-start(bf16[12,4,512]{2,1,0:T(4,128)(2,1)S(1)} %get-tuple-element.23), channel_id=1, source_target_pairs={{0,64},{1,2},{2,1},{3,67},{4,68},{5,69},{6,70},{7,71},{8,72},{9,73... | collective-permute-start | bytes 147464 | tf_op jit(solution)/shard_map/ppermute | solution.py:341
  5.3 6.8 %copy-start.2 = (bf16[9,128,128]{2,1,0:T(8,128)(2,1)S(1)}, bf16[9,128,128]{2,1,0:T(8,128)(2,1)}, u32[]{:S(2)}) copy-start(bf16[9,128,128]{2,1,0:T(8,128)(2,1)} %wmid_raw.1) | copy-start | bytes 884740
  5.3 6.8 %copy-start.7 = (bf16[9,128,4]{1,2,0:T(4,128)(2,1)S(1)}, bf16[9,128,4]{1,2,0:T(4,128)(2,1)}, u32[]{:S(2)}) copy-start(bf16[9,128,4]{1,2,0:T(4,128)(2,1)} %param.19) | copy-start | bytes 27652
  5.4 6.8 %copy-start.8 = (bf16[9,4,128]{2,1,0:T(4,128)(2,1)S(1)}, bf16[9,4,128]{2,1,0:T(4,128)(2,1)}, u32[]{:S(2)}) copy-start(bf16[9,4,128]{2,1,0:T(4,128)(2,1)} %wout_raw.1) | copy-start | bytes 27652
  5.4 7.4 %collective-permute-start.2 = (bf16[12,4,512]{2,1,0:T(4,128)(2,1)S(1)}, bf16[12,4,512]{2,1,0:T(4,128)(2,1)S(1)}, u32[]{:S(2)}, u32[]{:S(2)}) collective-permute-start(bf16[12,4,512]{2,1,0:T(4,128)(2,1)S(1)} %get-tuple-element.21), channel_id=1, source_target_pairs={{0,64},{1,65},{2,63},{3,2},{4,3},{5,4},{6,5},{7,6},{8,7},{9,8},{10... | collective-permute-start | bytes 147464 | tf_op jit(solution)/shard_map/ppermute | solution.py:342
  12.2 0.9 %copy-start = (f32[2,4,8,512]{3,2,1,0:T(8,128)S(1)}, f32[2,4,8,512]{3,2,1,0:T(8,128)}, u32[]{:S(2)}) copy-start(f32[2,4,8,512]{3,2,1,0:T(8,128)} %x_ref.1) | copy-start | bytes 393220
  12.2 0.9 %copy-start.1 = (f32[4,8,512]{2,1,0:T(8,128)S(1)}, f32[4,8,512]{2,1,0:T(8,128)}, u32[]{:S(2)}) copy-start(f32[4,8,512]{2,1,0:T(8,128)} %obs_ref.1) | copy-start | bytes 196612
  12.2 1.0 %copy-start.3 = (f32[2,4,8,512]{3,2,1,0:T(8,128)S(1)}, f32[2,4,8,512]{3,2,1,0:T(8,128)}, u32[]{:S(2)}) copy-start(f32[2,4,8,512]{3,2,1,0:T(8,128)} %noise_ref.1) | copy-start | bytes 393220
  12.2 1.0 %copy-start.4 = (f32[4,8,512]{2,1,0:T(8,128)S(1)}, f32[4,8,512]{2,1,0:T(8,128)}, u32[]{:S(2)}) copy-start(f32[4,8,512]{2,1,0:T(8,128)} %start_ref.1) | copy-start | bytes 196612
  21.4 2.5 %collective-permute-start.3 = (bf16[4,8,512]{2,1,0:T(8,128)(2,1)S(1)}, bf16[4,8,512]{2,1,0:T(8,128)(2,1)S(1)}, u32[]{:S(2)}, u32[]{:S(2)}) collective-permute-start(bf16[4,8,512]{2,1,0:T(8,128)(2,1)S(1)} %get-tuple-element.20), channel_id=1, source_target_pairs={{0,64},{64,128},{128,192},{192,0},{1,65},{65,129},{129,193},{193,1... | collective-permute-start | bytes 98312 | tf_op jit(solution)/shard_map/ppermute | solution.py:400
  22.8 3.4 %collective-permute-start.4 = (bf16[4,8,512]{2,1,0:T(8,128)(2,1)S(1)}, bf16[4,8,512]{2,1,0:T(8,128)(2,1)S(1)}, u32[]{:S(2)}, u32[]{:S(2)}) collective-permute-start(bf16[4,8,512]{2,1,0:T(8,128)(2,1)S(1)} %get-tuple-element.20), channel_id=1, source_target_pairs={{0,128},{64,192},{128,0},{192,64},{1,129},{65,193},{129,1},{193,65... | collective-permute-start | bytes 98312 | tf_op jit(solution)/shard_map/ppermute | solution.py:400
  23.6 3.3 %collective-permute-start.5 = (bf16[4,8,512]{2,1,0:T(8,128)(2,1)S(1)}, bf16[4,8,512]{2,1,0:T(8,128)(2,1)S(1)}, u32[]{:S(2)}, u32[]{:S(2)}) collective-permute-start(bf16[4,8,512]{2,1,0:T(8,128)(2,1)S(1)} %get-tuple-element.20), channel_id=1, source_target_pairs={{0,192},{64,0},{128,64},{192,128},{1,193},{65,1},{129,65},{193,129... | collective-permute-start | bytes 98312 | tf_op jit(solution)/shard_map/ppermute | solution.py:400

commit v4 on v3

--- a/solution.py
+++ b/solution.py
@@ -396,9 +396,9 @@
     m = lax.axis_size("tm")
     me = lax.axis_index("tm")
     before = 0.0
-    for k in range(1, m):
-        part = lax.ppermute(tot, "tm", [(i, (i + k) % m) for i in range(m)])
-        before = before + jnp.where(me >= k, part.astype(F32), 0.0)
+    for k in reversed(range(1, m)):
+        part = lax.ppermute(tot, "tm", [(i, i ^ k) for i in range(m)])
+        before = before + jnp.where(me > (me ^ k), part.astype(F32), 0.0)
     return loc + before
 
 

time: 27.8 us -> 26.8 us (0.964)
  waiting for transfers between devices: 3.34 us -> 2.37 us
    ppermute x3, waiting for transfers between devices: 3.34 us -> 2.37 us  [per_device(): part = lax.ppermute(tot, 'tm', [(i, i ^ k) for i in range(m)])]
  transfers between devices with their start and end apart: 6 -> 6, of which waited for: 3 -> 2; matrix products, arithmetic and copies ran while one was open for 0% -> 0% of each run, Pallas kernels for 6% -> 6%
where the time goes in v4:
time: 26.8 us; the launch traced here: 26.7 us
  starting transfers between devices  11.9 us (44%)
  Pallas kernels  9.85 us (37%)
  waiting for transfers between devices  2.37 us (9%)
  other arithmetic  2 us (7%)
  local copies, waits for them, and re-layouts  0.46 us (2%)
    pallas_call x1, Pallas kernels, per_device(): pl.pallas_call(main_kernel, out_shape=(local, total), in_specs=[vmem] * 1...  8.18 us
    ppermute x1, starting transfers between devices, per_device(): got_b = lax.ppermute(send_b, both, up)  5.6 us
    ppermute x1, starting transfers between devices, per_device(): got_f = lax.ppermute(send_f, both, down)  3.07 us
    ppermute x3, waiting for transfers between devices, per_device(): part = lax.ppermute(tot, 'tm', [(i, i ^ k) for i in range(m)])  2.37 us
    ppermute x3, starting transfers between devices, per_device(): part = lax.ppermute(tot, 'tm', [(i, i ^ k) for i in range(m)])  2.27 us
    convert_element_type x1, other arithmetic, per_device(): send_b = head.astype(BF16)  1.31 us
    pallas_call x1, Pallas kernels, per_device(): pl.pallas_call(tables_kernel, out_shape=(jax.ShapeDtypeStruct((W, W), BF1...  1.17 us
    ppermute x1, starting transfers between devices, per_device(): got_s = lax.ppermute(send_s, both, swap)  0.96 us
  transfers between devices with their start and end apart: 6, of which 2 were waited for; matrix products, arithmetic and copies ran while one was open for 0% of the time, Pallas kernels for 6%

profile of v4, /device:TPU:7, one launch (start us, length us, event | category | flops | bytes accessed | tf_op | source)
XLA Modules:
  0.0 26.7 jit_solution(12460488969445051357)
XLA Ops:
  0.0 1.3 %fusion.1 = (bf16[12,4,512]{2,1,0:T(4,128)(2,1)S(1)}, bf16[12,4,512]{2,1,0:T(4,128)(2,1)S(1)}, bf16[12,4,512]{2,1,0:T(4,128)(2,1)S(1)}) fusion(f32[4,8,512]{2,1,0:T(8,128)} %obs_ref.1, f32[8,8,512]{2,1,0:T(8,128)} %bitcast.2, pred[]{:T(512)S(6)} %eq.3), kind=kLoop, calls=%fused_computation.8 | loop fusion | flops 442368 | bytes 344065 | tf_op jit(solution)/shard_map/convert_element_type | solution.py:336
  1.3 3.1 %collective-permute-start = (bf16[12,4,512]{2,1,0:T(4,128)(2,1)S(1)}, bf16[12,4,512]{2,1,0:T(4,128)(2,1)S(1)}, u32[]{:S(2)}, u32[]{:S(2)}) collective-permute-start(bf16[12,4,512]{2,1,0:T(4,128)(2,1)S(1)} %get-tuple-element.22), channel_id=1, source_target_pairs={{0,1},{1,0},{2,3},{3,4},{4,5},{5,6},{6,7},{7,8},{8,9},{9,10},{10,1... | collective-permute-start | bytes 147464 | tf_op jit(solution)/shard_map/ppermute | solution.py:340
  4.4 1.0 %collective-permute-start.1 = (bf16[12,4,512]{2,1,0:T(4,128)(2,1)S(1)}, bf16[12,4,512]{2,1,0:T(4,128)(2,1)S(1)}, u32[]{:S(2)}, u32[]{:S(2)}) collective-permute-start(bf16[12,4,512]{2,1,0:T(4,128)(2,1)S(1)} %get-tuple-element.23), channel_id=1, source_target_pairs={{0,64},{1,2},{2,1},{3,67},{4,68},{5,69},{6,70},{7,71},{8,72},{9,73... | collective-permute-start | bytes 147464 | tf_op jit(solution)/shard_map/ppermute | solution.py:341
  5.4 5.6 %collective-permute-start.2 = (bf16[12,4,512]{2,1,0:T(4,128)(2,1)S(1)}, bf16[12,4,512]{2,1,0:T(4,128)(2,1)S(1)}, u32[]{:S(2)}, u32[]{:S(2)}) collective-permute-start(bf16[12,4,512]{2,1,0:T(4,128)(2,1)S(1)} %get-tuple-element.21), channel_id=1, source_target_pairs={{0,64},{1,65},{2,63},{3,2},{4,3},{5,4},{6,5},{7,6},{8,7},{9,8},{10... | collective-permute-start | bytes 147464 | tf_op jit(solution)/shard_map/ppermute | solution.py:342
  11.0 0.0 copy-done.5
  11.0 0.0 copy-done.6
  11.0 0.0 copy-done.11
  11.0 0.0 copy-done.9
  11.0 0.0 copy-done.10
  11.0 1.2 %shard_map.118 = (bf16[512,512]{1,0:T(8,128)(2,1)S(1)}, f32[3,128,512]{2,1,0:T(8,128)S(1)}, f32[8,512]{1,0:T(8,128)S(1)}) custom-call(f32[16,4,25]{2,1,0:T(4,128)S(1)} %copy-done.5, s32[64,64]{1,0:T(8,128)S(1)} %copy-done.6, f32[2,128]{1,0:T(2,128)S(1)} %copy-done.9, f32[2]{0:T(128)S(1)} %copy-done.10, f32[2]{0:T(128)S(1)} %copy-done.11), custom_call_target="tpu_custom_call" | custom-call | flops 2000000000 | bytes 1000000 | tf_op jit(solution)/shard_map/pallas_call | solution.py:344
  12.1 0.0 copy-done.2
  12.2 0.0 copy-done.7
  12.2 0.0 copy-done.8
  12.2 0.0 copy-start
  12.2 0.0 copy-start.1
  12.2 0.0 copy-start.3
  12.2 0.0 copy-start.4
  12.2 0.5 %shard_map.119 = (bf16[6,256,256]{2,1,0:T(8,128)(2,1)S(1)}, bf16[1536,256]{1,0:T(8,128)(2,1)S(1)}, bf16[1280,128]{1,0:T(8,128)(2,1)S(1)}) custom-call(bf16[9,4,128]{2,1,0:T(4,128)(2,1)S(1)} %bitcast.3, bf16[9,128,128]{2,1,0:T(8,128)(2,1)S(1)} %copy-done.2, bf16[9,4,128]{2,1,0:T(4,128)(2,1)S(1)} %copy-done.8, f32[8,512]{1,0:T(8,128)S(1)} %get-tuple-element.13.rate_ref), custom_call_target="tpu_custom_call" | custom-call | flops 2000000000 | bytes 1000000 | tf_op jit(solution)/shard_map/pallas_call | solution.py:357
  12.7 0.0 collective-permute-done.f_ref
  12.7 0.0 collective-permute-done.1.s_ref
  12.8 0.0 collective-permute-done.2.b_ref
  12.8 0.3 %copy-done = f32[2,4,8,512]{3,2,1,0:T(8,128)S(1)} copy-done((f32[2,4,8,512]{3,2,1,0:T(8,128)S(1)}, f32[2,4,8,512]{3,2,1,0:T(8,128)}, u32[]{:S(2)}) %copy-start) | copy-done | bytes 131096
  13.1 0.0 copy-done.1
  13.1 0.1 copy-done.3
  13.2 8.2 %shard_map.120 = (f32[2,4,8,512]{3,2,1,0:T(8,128)S(1)}, bf16[4,8,512]{2,1,0:T(8,128)(2,1)S(1)}) custom-call(f32[2,4,8,512]{3,2,1,0:T(8,128)S(1)} %copy-done, f32[2,4,8,512]{3,2,1,0:T(8,128)S(1)} %copy-done.3, f32[4,8,512]{2,1,0:T(8,128)S(1)} %copy-done.4, f32[4,8,512]{2,1,0:T(8,128)S(1)} %copy-done.1, bf16[12,4,512]{2,1,0:T(4,128)(2,1)S(1)} %collective-permute-done.f_ref, ...), custom_call_target="tpu_custom_call" | custom-call | flops 8000000000 | bytes 1000000 | tf_op jit(solution)/shard_map/pallas_call | solution.py:376
  21.4 1.5 %collective-permute-start.3 = (bf16[4,8,512]{2,1,0:T(8,128)(2,1)S(1)}, bf16[4,8,512]{2,1,0:T(8,128)(2,1)S(1)}, u32[]{:S(2)}, u32[]{:S(2)}) collective-permute-start(bf16[4,8,512]{2,1,0:T(8,128)(2,1)S(1)} %get-tuple-element.20), channel_id=1, source_target_pairs={{0,192},{64,128},{128,64},{192,0},{1,193},{65,129},{129,65},{193,1... | collective-permute-start | bytes 98312 | tf_op jit(solution)/shard_map/ppermute | solution.py:400
  22.8 0.8 %collective-permute-start.4 = (bf16[4,8,512]{2,1,0:T(8,128)(2,1)S(1)}, bf16[4,8,512]{2,1,0:T(8,128)(2,1)S(1)}, u32[]{:S(2)}, u32[]{:S(2)}) collective-permute-start(bf16[4,8,512]{2,1,0:T(8,128)(2,1)S(1)} %get-tuple-element.20), channel_id=1, source_target_pairs={{0,128},{64,192},{128,0},{192,64},{1,129},{65,193},{129,1},{193,65... | collective-permute-start | bytes 98312 | tf_op jit(solution)/shard_map/ppermute | solution.py:400
  23.6 0.0 collective-permute-start.5
  23.6 1.7 %collective-permute-done.3 = bf16[4,8,512]{2,1,0:T(8,128)(2,1)S(1)} collective-permute-done((bf16[4,8,512]{2,1,0:T(8,128)(2,1)S(1)}, bf16[4,8,512]{2,1,0:T(8,128)(2,1)S(1)}, u32[]{:S(2)}, u32[]{:S(2)}) %collective-permute-start.3) | collective-permute-done | bytes 32800 | tf_op jit(solution)/shard_map/ppermute | solution.py:400
  25.3 0.7 %collective-permute-done.4 = bf16[4,8,512]{2,1,0:T(8,128)(2,1)S(1)} collective-permute-done((bf16[4,8,512]{2,1,0:T(8,128)(2,1)S(1)}, bf16[4,8,512]{2,1,0:T(8,128)(2,1)S(1)}, u32[]{:S(2)}, u32[]{:S(2)}) %collective-permute-start.4) | collective-permute-done | bytes 32800 | tf_op jit(solution)/shard_map/ppermute | solution.py:400
  26.0 0.0 collective-permute-done.5
  26.0 0.7 %broadcast_add_fusion = f32[2,4,8,512]{3,2,1,0:T(8,128)} fusion(f32[2,4,8,512]{3,2,1,0:T(8,128)S(1)} %get-tuple-element.19, f32[4,8,512]{2,1,0:T(8,128)S(1)} %select_add_fusion), kind=kLoop, calls=%fused_computation.6 | loop fusion | flops 32768 | bytes 327680 | tf_op jit(solution)/shard_map/add | solution.py:402
  (10 shorter events, 0.0 us)
Async XLA Ops:
  0.0 11.0 %copy-start.5 = (f32[16,4,25]{2,1,0:T(4,128)S(1)}, f32[16,4,25]{2,1,0:T(4,128)}, u32[]{:S(2)}) copy-start(f32[16,4,25]{2,1,0:T(4,128)} %psf_ref.1) | copy-start | bytes 19204
  0.0 11.0 %copy-start.6 = (s32[64,64]{1,0:T(8,128)S(1)}, s32[64,64]{1,0:T(8,128)}, u32[]{:S(2)}) copy-start(s32[64,64]{1,0:T(8,128)} %map_ref.1) | copy-start | bytes 49156
  1.3 11.4 %collective-permute-start = (bf16[12,4,512]{2,1,0:T(4,128)(2,1)S(1)}, bf16[12,4,512]{2,1,0:T(4,128)(2,1)S(1)}, u32[]{:S(2)}, u32[]{:S(2)}) collective-permute-start(bf16[12,4,512]{2,1,0:T(4,128)(2,1)S(1)} %get-tuple-element.22), channel_id=1, source_target_pairs={{0,1},{1,0},{2,3},{3,4},{4,5},{5,6},{6,7},{7,8},{8,9},{9,10},{10,1... | collective-permute-start | bytes 147464 | tf_op jit(solution)/shard_map/ppermute | solution.py:340
  4.4 6.6 %copy-start.11 = (f32[2]{0:T(128)S(1)}, f32[2]{0:T(128)}, u32[]{:S(2)}) copy-start(f32[2]{0:T(128)} %scale_ref.1) | copy-start | bytes 28
  4.4 6.6 %copy-start.9 = (f32[2,128]{1,0:T(2,128)S(1)}, f32[2,128]{1,0:T(2,128)}, u32[]{:S(2)}) copy-start(f32[2,128]{1,0:T(2,128)} %bias_ref.1) | copy-start | bytes 3076
  4.4 6.6 %copy-start.10 = (f32[2]{0:T(128)S(1)}, f32[2]{0:T(128)}, u32[]{:S(2)}) copy-start(f32[2]{0:T(128)} %step_ref.1) | copy-start | bytes 28
  4.4 8.4 %collective-permute-start.1 = (bf16[12,4,512]{2,1,0:T(4,128)(2,1)S(1)}, bf16[12,4,512]{2,1,0:T(4,128)(2,1)S(1)}, u32[]{:S(2)}, u32[]{:S(2)}) collective-permute-start(bf16[12,4,512]{2,1,0:T(4,128)(2,1)S(1)} %get-tuple-element.23), channel_id=1, source_target_pairs={{0,64},{1,2},{2,1},{3,67},{4,68},{5,69},{6,70},{7,71},{8,72},{9,73... | collective-permute-start | bytes 147464 | tf_op jit(solution)/shard_map/ppermute | solution.py:341
  5.3 6.8 %copy-start.2 = (bf16[9,128,128]{2,1,0:T(8,128)(2,1)S(1)}, bf16[9,128,128]{2,1,0:T(8,128)(2,1)}, u32[]{:S(2)}) copy-start(bf16[9,128,128]{2,1,0:T(8,128)(2,1)} %wmid_raw.1) | copy-start | bytes 884740
  5.3 6.8 %copy-start.7 = (bf16[9,128,4]{1,2,0:T(4,128)(2,1)S(1)}, bf16[9,128,4]{1,2,0:T(4,128)(2,1)}, u32[]{:S(2)}) copy-start(bf16[9,128,4]{1,2,0:T(4,128)(2,1)} %param.19) | copy-start | bytes 27652
  5.4 6.8 %copy-start.8 = (bf16[9,4,128]{2,1,0:T(4,128)(2,1)S(1)}, bf16[9,4,128]{2,1,0:T(4,128)(2,1)}, u32[]{:S(2)}) copy-start(bf16[9,4,128]{2,1,0:T(4,128)(2,1)} %wout_raw.1) | copy-start | bytes 27652
  5.4 7.4 %collective-permute-start.2 = (bf16[12,4,512]{2,1,0:T(4,128)(2,1)S(1)}, bf16[12,4,512]{2,1,0:T(4,128)(2,1)S(1)}, u32[]{:S(2)}, u32[]{:S(2)}) collective-permute-start(bf16[12,4,512]{2,1,0:T(4,128)(2,1)S(1)} %get-tuple-element.21), channel_id=1, source_target_pairs={{0,64},{1,65},{2,63},{3,2},{4,3},{5,4},{6,5},{7,6},{8,7},{9,8},{10... | collective-permute-start | bytes 147464 | tf_op jit(solution)/shard_map/ppermute | solution.py:342
  12.2 0.9 %copy-start = (f32[2,4,8,512]{3,2,1,0:T(8,128)S(1)}, f32[2,4,8,512]{3,2,1,0:T(8,128)}, u32[]{:S(2)}) copy-start(f32[2,4,8,512]{3,2,1,0:T(8,128)} %x_ref.1) | copy-start | bytes 393220
  12.2 0.9 %copy-start.1 = (f32[4,8,512]{2,1,0:T(8,128)S(1)}, f32[4,8,512]{2,1,0:T(8,128)}, u32[]{:S(2)}) copy-start(f32[4,8,512]{2,1,0:T(8,128)} %obs_ref.1) | copy-start | bytes 196612
  12.2 1.0 %copy-start.3 = (f32[2,4,8,512]{3,2,1,0:T(8,128)S(1)}, f32[2,4,8,512]{3,2,1,0:T(8,128)}, u32[]{:S(2)}) copy-start(f32[2,4,8,512]{3,2,1,0:T(8,128)} %noise_ref.1) | copy-start | bytes 393220
  12.2 1.0 %copy-start.4 = (f32[4,8,512]{2,1,0:T(8,128)S(1)}, f32[4,8,512]{2,1,0:T(8,128)}, u32[]{:S(2)}) copy-start(f32[4,8,512]{2,1,0:T(8,128)} %start_ref.1) | copy-start | bytes 196612
  21.4 3.9 %collective-permute-start.3 = (bf16[4,8,512]{2,1,0:T(8,128)(2,1)S(1)}, bf16[4,8,512]{2,1,0:T(8,128)(2,1)S(1)}, u32[]{:S(2)}, u32[]{:S(2)}) collective-permute-start(bf16[4,8,512]{2,1,0:T(8,128)(2,1)S(1)} %get-tuple-element.20), channel_id=1, source_target_pairs={{0,192},{64,128},{128,64},{192,0},{1,193},{65,129},{129,65},{193,1... | collective-permute-start | bytes 98312 | tf_op jit(solution)/shard_map/ppermute | solution.py:400
  22.8 3.2 %collective-permute-start.4 = (bf16[4,8,512]{2,1,0:T(8,128)(2,1)S(1)}, bf16[4,8,512]{2,1,0:T(8,128)(2,1)S(1)}, u32[]{:S(2)}, u32[]{:S(2)}) collective-permute-start(bf16[4,8,512]{2,1,0:T(8,128)(2,1)S(1)} %get-tuple-element.20), channel_id=1, source_target_pairs={{0,128},{64,192},{128,0},{192,64},{1,129},{65,193},{129,1},{193,65... | collective-permute-start | bytes 98312 | tf_op jit(solution)/shard_map/ppermute | solution.py:400
  23.6 2.4 %collective-permute-start.5 = (bf16[4,8,512]{2,1,0:T(8,128)(2,1)S(1)}, bf16[4,8,512]{2,1,0:T(8,128)(2,1)S(1)}, u32[]{:S(2)}, u32[]{:S(2)}) collective-permute-start(bf16[4,8,512]{2,1,0:T(8,128)(2,1)S(1)} %get-tuple-element.20), channel_id=1, source_target_pairs={{0,64},{64,0},{128,192},{192,128},{1,65},{65,1},{129,193},{193,129... | collective-permute-start | bytes 98312 | tf_op jit(solution)/shard_map/ppermute | solution.py:400

commit v5 on v4

--- a/solution.py
+++ b/solution.py
@@ -261,7 +261,8 @@
         both = dot(h2[t], wout_ref[...])
         high = both.astype(BF16)
         low = (both - high.astype(F32)).astype(BF16)
-        product[t] = dot_tn(high, perm[...]) + dot_tn(low, perm[...])
+        moved = dot_tn(jnp.concatenate([high, low], axis=1), perm[...])
+        product[t] = moved[:C] + moved[C:]
 
     running = [None] * B
 

time: 26.8 us -> 26.5 us (0.989)
  Pallas kernels: 9.85 us -> 9.56 us
    pallas_call x1, Pallas kernels: 8.18 us -> 7.88 us  [per_device(): pl.pallas_call(main_kernel, out_shape=(local, total), in_specs=[vmem] * 1...]
where the time goes in v5:
time: 26.5 us; the launch traced here: 26.4 us
  starting transfers between devices  11.9 us (45%)
  Pallas kernels  9.56 us (36%)
  waiting for transfers between devices  2.38 us (9%)
  other arithmetic  2 us (8%)
  local copies, waits for them, and re-layouts  0.46 us (2%)
    pallas_call x1, Pallas kernels, per_device(): pl.pallas_call(main_kernel, out_shape=(local, total), in_specs=[vmem] * 1...  7.88 us
    ppermute x1, starting transfers between devices, per_device(): got_b = lax.ppermute(send_b, both, up)  5.6 us
    ppermute x1, starting transfers between devices, per_device(): got_f = lax.ppermute(send_f, both, down)  3.07 us
    ppermute x3, waiting for transfers between devices, per_device(): part = lax.ppermute(tot, 'tm', [(i, i ^ k) for i in range(m)])  2.37 us
    ppermute x3, starting transfers between devices, per_device(): part = lax.ppermute(tot, 'tm', [(i, i ^ k) for i in range(m)])  2.27 us
    convert_element_type x1, other arithmetic, per_device(): send_b = head.astype(BF16)  1.31 us
    pallas_call x1, Pallas kernels, per_device(): pl.pallas_call(tables_kernel, out_shape=(jax.ShapeDtypeStruct((W, W), BF1...  1.17 us
    ppermute x1, starting transfers between devices, per_device(): got_s = lax.ppermute(send_s, both, swap)  0.96 us
  transfers between devices with their start and end apart: 6, of which 2 were waited for; matrix products, arithmetic and copies ran while one was open for 0% of the time, Pallas kernels for 6%

profile of v5, /device:TPU:7, one launch (start us, length us, event | category | flops | bytes accessed | tf_op | source)
XLA Modules:
  0.0 26.4 jit_solution(10647081786218194358)
XLA Ops:
  0.0 1.3 %fusion.1 = (bf16[12,4,512]{2,1,0:T(4,128)(2,1)S(1)}, bf16[12,4,512]{2,1,0:T(4,128)(2,1)S(1)}, bf16[12,4,512]{2,1,0:T(4,128)(2,1)S(1)}) fusion(f32[4,8,512]{2,1,0:T(8,128)} %obs_ref.1, f32[8,8,512]{2,1,0:T(8,128)} %bitcast.2, pred[]{:T(512)S(6)} %eq.3), kind=kLoop, calls=%fused_computation.8 | loop fusion | flops 442368 | bytes 344065 | tf_op jit(solution)/shard_map/convert_element_type | solution.py:337
  1.3 3.1 %collective-permute-start = (bf16[12,4,512]{2,1,0:T(4,128)(2,1)S(1)}, bf16[12,4,512]{2,1,0:T(4,128)(2,1)S(1)}, u32[]{:S(2)}, u32[]{:S(2)}) collective-permute-start(bf16[12,4,512]{2,1,0:T(4,128)(2,1)S(1)} %get-tuple-element.22), channel_id=1, source_target_pairs={{0,1},{1,0},{2,3},{3,4},{4,5},{5,6},{6,7},{7,8},{8,9},{9,10},{10,1... | collective-permute-start | bytes 147464 | tf_op jit(solution)/shard_map/ppermute | solution.py:341
  4.4 1.0 %collective-permute-start.1 = (bf16[12,4,512]{2,1,0:T(4,128)(2,1)S(1)}, bf16[12,4,512]{2,1,0:T(4,128)(2,1)S(1)}, u32[]{:S(2)}, u32[]{:S(2)}) collective-permute-start(bf16[12,4,512]{2,1,0:T(4,128)(2,1)S(1)} %get-tuple-element.23), channel_id=1, source_target_pairs={{0,64},{1,2},{2,1},{3,67},{4,68},{5,69},{6,70},{7,71},{8,72},{9,73... | collective-permute-start | bytes 147464 | tf_op jit(solution)/shard_map/ppermute | solution.py:342
  5.4 5.6 %collective-permute-start.2 = (bf16[12,4,512]{2,1,0:T(4,128)(2,1)S(1)}, bf16[12,4,512]{2,1,0:T(4,128)(2,1)S(1)}, u32[]{:S(2)}, u32[]{:S(2)}) collective-permute-start(bf16[12,4,512]{2,1,0:T(4,128)(2,1)S(1)} %get-tuple-element.21), channel_id=1, source_target_pairs={{0,64},{1,65},{2,63},{3,2},{4,3},{5,4},{6,5},{7,6},{8,7},{9,8},{10... | collective-permute-start | bytes 147464 | tf_op jit(solution)/shard_map/ppermute | solution.py:343
  11.0 0.0 copy-done.5
  11.0 0.0 copy-done.6
  11.0 0.0 copy-done.11
  11.0 0.0 copy-done.9
  11.0 0.0 copy-done.10
  11.0 1.2 %shard_map.118 = (bf16[512,512]{1,0:T(8,128)(2,1)S(1)}, f32[3,128,512]{2,1,0:T(8,128)S(1)}, f32[8,512]{1,0:T(8,128)S(1)}) custom-call(f32[16,4,25]{2,1,0:T(4,128)S(1)} %copy-done.5, s32[64,64]{1,0:T(8,128)S(1)} %copy-done.6, f32[2,128]{1,0:T(2,128)S(1)} %copy-done.9, f32[2]{0:T(128)S(1)} %copy-done.10, f32[2]{0:T(128)S(1)} %copy-done.11), custom_call_target="tpu_custom_call" | custom-call | flops 2000000000 | bytes 1000000 | tf_op jit(solution)/shard_map/pallas_call | solution.py:345
  12.1 0.0 copy-done.2
  12.2 0.0 copy-done.7
  12.2 0.0 copy-done.8
  12.2 0.0 copy-start
  12.2 0.0 copy-start.1
  12.2 0.0 copy-start.3
  12.2 0.0 copy-start.4
  12.2 0.5 %shard_map.119 = (bf16[6,256,256]{2,1,0:T(8,128)(2,1)S(1)}, bf16[1536,256]{1,0:T(8,128)(2,1)S(1)}, bf16[1280,128]{1,0:T(8,128)(2,1)S(1)}) custom-call(bf16[9,4,128]{2,1,0:T(4,128)(2,1)S(1)} %bitcast.3, bf16[9,128,128]{2,1,0:T(8,128)(2,1)S(1)} %copy-done.2, bf16[9,4,128]{2,1,0:T(4,128)(2,1)S(1)} %copy-done.8, f32[8,512]{1,0:T(8,128)S(1)} %get-tuple-element.13.rate_ref), custom_call_target="tpu_custom_call" | custom-call | flops 2000000000 | bytes 1000000 | tf_op jit(solution)/shard_map/pallas_call | solution.py:358
  12.7 0.0 collective-permute-done.f_ref
  12.7 0.0 collective-permute-done.1.s_ref
  12.8 0.0 collective-permute-done.2.b_ref
  12.8 0.3 %copy-done = f32[2,4,8,512]{3,2,1,0:T(8,128)S(1)} copy-done((f32[2,4,8,512]{3,2,1,0:T(8,128)S(1)}, f32[2,4,8,512]{3,2,1,0:T(8,128)}, u32[]{:S(2)}) %copy-start) | copy-done | bytes 131096
  13.1 0.0 copy-done.1
  13.1 0.1 copy-done.3
  13.2 7.9 %shard_map.120 = (f32[2,4,8,512]{3,2,1,0:T(8,128)S(1)}, bf16[4,8,512]{2,1,0:T(8,128)(2,1)S(1)}) custom-call(f32[2,4,8,512]{3,2,1,0:T(8,128)S(1)} %copy-done, f32[2,4,8,512]{3,2,1,0:T(8,128)S(1)} %copy-done.3, f32[4,8,512]{2,1,0:T(8,128)S(1)} %copy-done.4, f32[4,8,512]{2,1,0:T(8,128)S(1)} %copy-done.1, bf16[12,4,512]{2,1,0:T(4,128)(2,1)S(1)} %collective-permute-done.f_ref, ...), custom_call_target="tpu_custom_call" | custom-call | flops 8000000000 | bytes 1000000 | tf_op jit(solution)/shard_map/pallas_call | solution.py:377
  21.1 1.5 %collective-permute-start.3 = (bf16[4,8,512]{2,1,0:T(8,128)(2,1)S(1)}, bf16[4,8,512]{2,1,0:T(8,128)(2,1)S(1)}, u32[]{:S(2)}, u32[]{:S(2)}) collective-permute-start(bf16[4,8,512]{2,1,0:T(8,128)(2,1)S(1)} %get-tuple-element.20), channel_id=1, source_target_pairs={{0,192},{64,128},{128,64},{192,0},{1,193},{65,129},{129,65},{193,1... | collective-permute-start | bytes 98312 | tf_op jit(solution)/shard_map/ppermute | solution.py:401
  22.5 0.8 %collective-permute-start.4 = (bf16[4,8,512]{2,1,0:T(8,128)(2,1)S(1)}, bf16[4,8,512]{2,1,0:T(8,128)(2,1)S(1)}, u32[]{:S(2)}, u32[]{:S(2)}) collective-permute-start(bf16[4,8,512]{2,1,0:T(8,128)(2,1)S(1)} %get-tuple-element.20), channel_id=1, source_target_pairs={{0,128},{64,192},{128,0},{192,64},{1,129},{65,193},{129,1},{193,65... | collective-permute-start | bytes 98312 | tf_op jit(solution)/shard_map/ppermute | solution.py:401
  23.3 0.0 collective-permute-start.5
  23.3 1.7 %collective-permute-done.3 = bf16[4,8,512]{2,1,0:T(8,128)(2,1)S(1)} collective-permute-done((bf16[4,8,512]{2,1,0:T(8,128)(2,1)S(1)}, bf16[4,8,512]{2,1,0:T(8,128)(2,1)S(1)}, u32[]{:S(2)}, u32[]{:S(2)}) %collective-permute-start.3) | collective-permute-done | bytes 32800 | tf_op jit(solution)/shard_map/ppermute | solution.py:401
  25.0 0.7 %collective-permute-done.4 = bf16[4,8,512]{2,1,0:T(8,128)(2,1)S(1)} collective-permute-done((bf16[4,8,512]{2,1,0:T(8,128)(2,1)S(1)}, bf16[4,8,512]{2,1,0:T(8,128)(2,1)S(1)}, u32[]{:S(2)}, u32[]{:S(2)}) %collective-permute-start.4) | collective-permute-done | bytes 32800 | tf_op jit(solution)/shard_map/ppermute | solution.py:401
  25.7 0.0 collective-permute-done.5
  25.7 0.7 %broadcast_add_fusion = f32[2,4,8,512]{3,2,1,0:T(8,128)} fusion(f32[2,4,8,512]{3,2,1,0:T(8,128)S(1)} %get-tuple-element.19, f32[4,8,512]{2,1,0:T(8,128)S(1)} %select_add_fusion), kind=kLoop, calls=%fused_computation.6 | loop fusion | flops 32768 | bytes 327680 | tf_op jit(solution)/shard_map/add | solution.py:403
  (10 shorter events, 0.0 us)
Async XLA Ops:
  0.0 11.0 %copy-start.5 = (f32[16,4,25]{2,1,0:T(4,128)S(1)}, f32[16,4,25]{2,1,0:T(4,128)}, u32[]{:S(2)}) copy-start(f32[16,4,25]{2,1,0:T(4,128)} %psf_ref.1) | copy-start | bytes 19204
  0.0 11.0 %copy-start.6 = (s32[64,64]{1,0:T(8,128)S(1)}, s32[64,64]{1,0:T(8,128)}, u32[]{:S(2)}) copy-start(s32[64,64]{1,0:T(8,128)} %map_ref.1) | copy-start | bytes 49156
  1.3 11.4 %collective-permute-start = (bf16[12,4,512]{2,1,0:T(4,128)(2,1)S(1)}, bf16[12,4,512]{2,1,0:T(4,128)(2,1)S(1)}, u32[]{:S(2)}, u32[]{:S(2)}) collective-permute-start(bf16[12,4,512]{2,1,0:T(4,128)(2,1)S(1)} %get-tuple-element.22), channel_id=1, source_target_pairs={{0,1},{1,0},{2,3},{3,4},{4,5},{5,6},{6,7},{7,8},{8,9},{9,10},{10,1... | collective-permute-start | bytes 147464 | tf_op jit(solution)/shard_map/ppermute | solution.py:341
  4.4 6.6 %copy-start.11 = (f32[2]{0:T(128)S(1)}, f32[2]{0:T(128)}, u32[]{:S(2)}) copy-start(f32[2]{0:T(128)} %scale_ref.1) | copy-start | bytes 28
  4.4 6.6 %copy-start.9 = (f32[2,128]{1,0:T(2,128)S(1)}, f32[2,128]{1,0:T(2,128)}, u32[]{:S(2)}) copy-start(f32[2,128]{1,0:T(2,128)} %bias_ref.1) | copy-start | bytes 3076
  4.4 6.6 %copy-start.10 = (f32[2]{0:T(128)S(1)}, f32[2]{0:T(128)}, u32[]{:S(2)}) copy-start(f32[2]{0:T(128)} %step_ref.1) | copy-start | bytes 28
  4.4 8.4 %collective-permute-start.1 = (bf16[12,4,512]{2,1,0:T(4,128)(2,1)S(1)}, bf16[12,4,512]{2,1,0:T(4,128)(2,1)S(1)}, u32[]{:S(2)}, u32[]{:S(2)}) collective-permute-start(bf16[12,4,512]{2,1,0:T(4,128)(2,1)S(1)} %get-tuple-element.23), channel_id=1, source_target_pairs={{0,64},{1,2},{2,1},{3,67},{4,68},{5,69},{6,70},{7,71},{8,72},{9,73... | collective-permute-start | bytes 147464 | tf_op jit(solution)/shard_map/ppermute | solution.py:342
  5.3 6.8 %copy-start.2 = (bf16[9,128,128]{2,1,0:T(8,128)(2,1)S(1)}, bf16[9,128,128]{2,1,0:T(8,128)(2,1)}, u32[]{:S(2)}) copy-start(bf16[9,128,128]{2,1,0:T(8,128)(2,1)} %wmid_raw.1) | copy-start | bytes 884740
  5.3 6.8 %copy-start.7 = (bf16[9,128,4]{1,2,0:T(4,128)(2,1)S(1)}, bf16[9,128,4]{1,2,0:T(4,128)(2,1)}, u32[]{:S(2)}) copy-start(bf16[9,128,4]{1,2,0:T(4,128)(2,1)} %param.19) | copy-start | bytes 27652
  5.4 6.8 %copy-start.8 = (bf16[9,4,128]{2,1,0:T(4,128)(2,1)S(1)}, bf16[9,4,128]{2,1,0:T(4,128)(2,1)}, u32[]{:S(2)}) copy-start(bf16[9,4,128]{2,1,0:T(4,128)(2,1)} %wout_raw.1) | copy-start | bytes 27652
  5.4 7.4 %collective-permute-start.2 = (bf16[12,4,512]{2,1,0:T(4,128)(2,1)S(1)}, bf16[12,4,512]{2,1,0:T(4,128)(2,1)S(1)}, u32[]{:S(2)}, u32[]{:S(2)}) collective-permute-start(bf16[12,4,512]{2,1,0:T(4,128)(2,1)S(1)} %get-tuple-element.21), channel_id=1, source_target_pairs={{0,64},{1,65},{2,63},{3,2},{4,3},{5,4},{6,5},{7,6},{8,7},{9,8},{10... | collective-permute-start | bytes 147464 | tf_op jit(solution)/shard_map/ppermute | solution.py:343
  12.2 0.9 %copy-start = (f32[2,4,8,512]{3,2,1,0:T(8,128)S(1)}, f32[2,4,8,512]{3,2,1,0:T(8,128)}, u32[]{:S(2)}) copy-start(f32[2,4,8,512]{3,2,1,0:T(8,128)} %x_ref.1) | copy-start | bytes 393220
  12.2 0.9 %copy-start.1 = (f32[4,8,512]{2,1,0:T(8,128)S(1)}, f32[4,8,512]{2,1,0:T(8,128)}, u32[]{:S(2)}) copy-start(f32[4,8,512]{2,1,0:T(8,128)} %obs_ref.1) | copy-start | bytes 196612
  12.2 1.0 %copy-start.3 = (f32[2,4,8,512]{3,2,1,0:T(8,128)S(1)}, f32[2,4,8,512]{3,2,1,0:T(8,128)}, u32[]{:S(2)}) copy-start(f32[2,4,8,512]{3,2,1,0:T(8,128)} %noise_ref.1) | copy-start | bytes 393220
  12.2 1.0 %copy-start.4 = (f32[4,8,512]{2,1,0:T(8,128)S(1)}, f32[4,8,512]{2,1,0:T(8,128)}, u32[]{:S(2)}) copy-start(f32[4,8,512]{2,1,0:T(8,128)} %start_ref.1) | copy-start | bytes 196612
  21.1 3.9 %collective-permute-start.3 = (bf16[4,8,512]{2,1,0:T(8,128)(2,1)S(1)}, bf16[4,8,512]{2,1,0:T(8,128)(2,1)S(1)}, u32[]{:S(2)}, u32[]{:S(2)}) collective-permute-start(bf16[4,8,512]{2,1,0:T(8,128)(2,1)S(1)} %get-tuple-element.20), channel_id=1, source_target_pairs={{0,192},{64,128},{128,64},{192,0},{1,193},{65,129},{129,65},{193,1... | collective-permute-start | bytes 98312 | tf_op jit(solution)/shard_map/ppermute | solution.py:401
  22.5 3.2 %collective-permute-start.4 = (bf16[4,8,512]{2,1,0:T(8,128)(2,1)S(1)}, bf16[4,8,512]{2,1,0:T(8,128)(2,1)S(1)}, u32[]{:S(2)}, u32[]{:S(2)}) collective-permute-start(bf16[4,8,512]{2,1,0:T(8,128)(2,1)S(1)} %get-tuple-element.20), channel_id=1, source_target_pairs={{0,128},{64,192},{128,0},{192,64},{1,129},{65,193},{129,1},{193,65... | collective-permute-start | bytes 98312 | tf_op jit(solution)/shard_map/ppermute | solution.py:401
  23.3 2.4 %collective-permute-start.5 = (bf16[4,8,512]{2,1,0:T(8,128)(2,1)S(1)}, bf16[4,8,512]{2,1,0:T(8,128)(2,1)S(1)}, u32[]{:S(2)}, u32[]{:S(2)}) collective-permute-start(bf16[4,8,512]{2,1,0:T(8,128)(2,1)S(1)} %get-tuple-element.20), channel_id=1, source_target_pairs={{0,64},{64,0},{128,192},{192,128},{1,65},{65,1},{129,193},{193,129... | collective-permute-start | bytes 98312 | tf_op jit(solution)/shard_map/ppermute | solution.py:401
